TPU v7x, 256 devices: a whole 4x4x8 slice. The times are simulated.
256 devices in a mesh: gx: 32 (over x, z), gy: 8 (over y, core).
Axes of the slice: x: 4, y: 4, z: 8, core: 2. Of those that a mesh axis runs over, the one named last changes fastest.
Arguments:
- probes: bfloat16 [64, 256, 128, 128], P(None, 'gx', 'gy'), may hold values from -6 to 6
- permeability: float32 [256, 128, 128], P('gx', 'gy'), may hold values from 0.2 to 5
- absorption: float32 [256, 128, 128], P('gx', 'gy'), may hold values from 0.3 to 3
- sensitivity: float32 [256, 128, 128], P('gx', 'gy'), may hold values from -6 to 6
- observe_weight: float32 [256, 128, 128], P('gx', 'gy'), may hold values from 1 to 10
Outputs:
- q_basis: float32 [64, 256, 128, 128], P(None, 'gx', 'gy')
- r_factor: float32 [64, 64], replicated
All inputs are finite; a program needn't handle non-finite values.
Results may differ from a plain program's by a relative error of at most 0.0003.
Values sent between devices are 32-bit elements; how exact they have to be, the bound alone decides.
A program may use at most 128 MiB of HBM per device.

v0:
```python
import jax
import jax.numpy as jnp
from jax import lax
from jax.sharding import PartitionSpec as P

SWEEPS = 4


def padded_2(shard, sides, width):
    for axis, dim in sides:
        peers, length = (lax.axis_size(axis), shard.shape[dim])
        up = [(i, (i + 1) % peers) for i in range(peers - 1)]
        down = [(j, i) for i, j in up]
        last = lax.slice_in_dim(shard, length - width, length, axis=dim)
        first = lax.slice_in_dim(shard, 0, width, axis=dim)
        before = lax.ppermute(last, axis, up)
        after = lax.ppermute(first, axis, down)
        shard = jnp.concatenate([before, shard, after], axis=dim)
    return shard


def face_terms(kpad, absorption):
    center = kpad[1:-1, 1:-1]
    x_low = 0.5 * (center + kpad[:-2, 1:-1])
    x_high = 0.5 * (center + kpad[2:, 1:-1])
    y_low = 0.5 * (center + kpad[1:-1, :-2])
    y_high = 0.5 * (center + kpad[1:-1, 2:])
    zpad = jnp.pad(center, ((0, 0), (0, 0), (1, 1)))
    z_low = 0.5 * (center + zpad[:, :, :-2])
    z_high = 0.5 * (center + zpad[:, :, 2:])
    diag = absorption + x_low + x_high + y_low + y_high + z_low + z_high
    return ((x_low, x_high, y_low, y_high, z_low, z_high), diag)


def sweep(field, padded, rhs, coefs, diag):
    x_low, x_high, y_low, y_high, z_low, z_high = coefs
    zpad = jnp.pad(field, ((0, 0), (0, 0), (0, 0), (1, 1)))
    total = x_low * padded[:, :-2, 1:-1] + x_high * padded[:, 2:, 1:-1]
    total = total + y_low * padded[:, 1:-1, :-2] + y_high * padded[:, 1:-1, 2:]
    total = total + z_low * zpad[..., :-2] + z_high * zpad[..., 2:]
    return 0.2 * field + 0.8 * (rhs + total) / diag


def single_solve(rhs, coefs, diag):
    field = 0.8 * rhs / diag
    for step in range(SWEEPS - 1):
        padded = padded_2(field, (("gx", 1), ("gy", 2)), 1)
        field = sweep(field, padded, rhs, coefs, diag)
    return field


def lower_inverse(lower):
    width = lower.shape[0]
    identity = jnp.eye(width, dtype=jnp.float32)

    def row_step(index, inverse):
        row = lax.dynamic_slice_in_dim(lower, index, 1, 0)
        pivot = lax.dynamic_slice(lower, (index, index), (1, 1))
        unit = lax.dynamic_slice_in_dim(identity, index, 1, 0)
        partial_sum = jnp.dot(
            row, inverse, precision=lax.Precision.HIGHEST, preferred_element_type=jnp.float32
        )
        new_row = (unit - partial_sum) / pivot
        return lax.dynamic_update_slice_in_dim(inverse, new_row, index, 0)

    return lax.fori_loop(0, width, row_step, jnp.zeros((width, width), jnp.float32))


def body(probes, permeability, absorption, sensitivity, observe_weight):
    count, width_x, width_y, width_z = probes.shape
    total_cells = width_x * lax.axis_size("gx") * width_y * lax.axis_size("gy") * width_z
    source = sensitivity * probes.astype(jnp.float32)
    kpad = padded_2(permeability, (("gx", 0), ("gy", 1)), 1)
    coefs, diag = face_terms(kpad, absorption)
    forward = single_solve(source, coefs, diag)
    adjoint = single_solve(observe_weight * forward, coefs, diag)
    responses = (sensitivity * adjoint).reshape(count, -1)
    gram = jnp.dot(
        responses, responses.T, precision=lax.Precision.HIGHEST, preferred_element_type=jnp.float32
    ) / float(total_cells)
    summed = lax.psum(gram, ("gx", "gy"))
    r_factor = jnp.linalg.cholesky(summed).T
    inverse = lower_inverse(r_factor.T)
    q_basis = jnp.dot(
        inverse, responses, precision=lax.Precision.HIGHEST, preferred_element_type=jnp.float32
    )
    return (q_basis.reshape(count, width_x, width_y, width_z), r_factor)


def solution(mesh):
    return jax.shard_map(
        body,
        mesh=mesh,
        in_specs=(
            P(None, "gx", "gy", None),
            P("gx", "gy", None),
            P("gx", "gy", None),
            P("gx", "gy", None),
            P("gx", "gy", None),
        ),
        out_specs=(P(None, "gx", "gy", None), P()),
        check_vma=False,
    )
```

profile of v0, /device:TPU:1, one launch (start us, length us, event | category | flops | bytes accessed | tf_op | source)
XLA Modules:
  0.0 477.7 jit_solution(5736251679478385338)
XLA Ops:
  1.3 4.4 collective-permute-start
  7.9 2.4 collective-permute-done.1
  10.3 5.0 %collective-permute-start.2 = (f32[10,1,128]{2,1,0:T(1,128)S(1)}, f32[10,1,128]{2,1,0:T(1,128)S(1)}, u32[]{:S(2)}, u32[]{:S(2)}) collective-permute-start(f32[10,1,128]{2,1,0:T(1,128)S(1)} %get-tuple-element.132), channel_id=1, source_target_pairs={{0,1},{1,2},{2,3},{3,4},{4,5},{5,6},{6,7},{8,9},{9,10},{10,11},{11... | collective-permute-start | bytes 15368 | tf_op jit(solution)/shard_map/ppermute | solution.py:16
  15.3 1.9 collective-permute-start.3
  17.3 3.0 collective-permute-done.3
  21.4 3.4 multiply_divide_fusion.1
  24.9 3.7 collective-permute-start.4
  28.6 1.3 collective-permute-start.5
  29.9 9.0 %collective-permute-done.4 = f32[64,1,16,128]{3,0,2,1:T(8,128)S(1)} collective-permute-done((f32[64,1,16,128]{3,0,2,1:T(8,128)S(1)}, f32[64,1,16,128]{3,0,2,1:T(8,128)S(1)}, u32[]{:S(2)}, u32[]{:S(2)}) %collective-permute-start.4) | collective-permute-done | bytes 524320 | tf_op jit(solution)/shard_map/ppermute | solution.py:16
  38.9 5.1 %collective-permute-done.5 = f32[64,1,16,128]{3,0,2,1:T(8,128)S(1)} collective-permute-done((f32[64,1,16,128]{3,0,2,1:T(8,128)S(1)}, f32[64,1,16,128]{3,0,2,1:T(8,128)S(1)}, u32[]{:S(2)}, u32[]{:S(2)}) %collective-permute-start.5) | collective-permute-done | bytes 524320 | tf_op jit(solution)/shard_map/ppermute | solution.py:17
  44.1 3.9 collective-permute-start.6
  48.0 1.9 collective-permute-start.7
  49.9 2.1 collective-permute-done.6
  52.0 4.4 collective-permute-done.7
  56.4 7.8 %fusion.10 = f32[64,8,16,128]{3,0,2,1:T(8,128)S(1)} fusion(f32[64,8,16,128]{3,0,2,1:T(8,128)S(1)} %multiply_divide_fusion.1, f32[64,10,1,128]{3,0,2,1:T(8,128)S(1)} %collective-permute-done.7, f32[64,1,16,128]{3,0,2,1:T(8,128)S(1)} %collective-permute-done.5, f32[64,1,16,128]{3,0,2,1:T(8,128)S(1)} %collective-permute-done.4, ...), kind=kLoop, calls=%fused_computation.23 | loop fusion | flops 27262976 | bytes 12713984 | tf_op jit(solution)/shard_map/add | solution.py:41
  64.3 4.9 %collective-permute-start.8 = (f32[64,1,16,128]{3,0,2,1:T(8,128)S(1)}, f32[64,1,16,128]{3,0,2,1:T(8,128)S(1)}, u32[]{:S(2)}, u32[]{:S(2)}) collective-permute-start(f32[64,1,16,128]{3,0,2,1:T(8,128)S(1)} %get-tuple-element.127), channel_id=1, source_target_pairs={{0,8},{8,16},{16,24},{24,32},{32,40},{40,48},{48,56},{56,64},{64,7... | collective-permute-start | bytes 1572872 | tf_op jit(solution)/shard_map/ppermute | solution.py:16
  70.5 6.0 %collective-permute-done.8 = f32[64,1,16,128]{3,0,2,1:T(8,128)S(1)} collective-permute-done((f32[64,1,16,128]{3,0,2,1:T(8,128)S(1)}, f32[64,1,16,128]{3,0,2,1:T(8,128)S(1)}, u32[]{:S(2)}, u32[]{:S(2)}) %collective-permute-start.8) | collective-permute-done | bytes 524320 | tf_op jit(solution)/shard_map/ppermute | solution.py:16
  76.5 4.4 collective-permute-done.9
  81.0 6.2 %collective-permute-start.10 = (f32[64,10,1,128]{3,0,2,1:T(8,128)S(1)}, f32[64,10,1,128]{3,0,2,1:T(8,128)S(1)}, u32[]{:S(2)}, u32[]{:S(2)}) collective-permute-start(f32[64,10,1,128]{3,0,2,1:T(8,128)S(1)} %get-tuple-element.115), channel_id=1, source_target_pairs={{0,1},{1,2},{2,3},{3,4},{4,5},{5,6},{6,7},{8,9},{9,10},{10,11},{11... | collective-permute-start | bytes 983048 | tf_op jit(solution)/shard_map/ppermute | solution.py:16
  87.2 1.9 collective-permute-start.11
  89.1 2.1 collective-permute-done.10
  91.2 4.4 collective-permute-done.11
  95.6 7.8 %fusion.18 = f32[64,8,16,128]{3,0,2,1:T(8,128)S(1)} fusion(f32[64,8,16,128]{3,0,2,1:T(8,128)S(1)} %fusion.10, f32[64,10,1,128]{3,0,2,1:T(8,128)S(1)} %collective-permute-done.11, f32[64,1,16,128]{3,0,2,1:T(8,128)S(1)} %collective-permute-done.9, f32[64,1,16,128]{3,0,2,1:T(8,128)S(1)} %collective-permute-done.8, ...), kind=kLoop, calls=%fused_computation.31 | loop fusion | flops 27262976 | bytes 12713984 | tf_op jit(solution)/shard_map/add | solution.py:41
  103.5 4.0 collective-permute-start.12
  108.8 6.0 %collective-permute-done.12 = f32[64,1,16,128]{3,0,2,1:T(8,128)S(1)} collective-permute-done((f32[64,1,16,128]{3,0,2,1:T(8,128)S(1)}, f32[64,1,16,128]{3,0,2,1:T(8,128)S(1)}, u32[]{:S(2)}, u32[]{:S(2)}) %collective-permute-start.12) | collective-permute-done | bytes 524320 | tf_op jit(solution)/shard_map/ppermute | solution.py:16
  114.8 4.1 collective-permute-done.13
  119.0 6.7 %collective-permute-start.14 = (f32[64,10,1,128]{3,0,2,1:T(8,128)S(1)}, f32[64,10,1,128]{3,0,2,1:T(8,128)S(1)}, u32[]{:S(2)}, u32[]{:S(2)}) collective-permute-start(f32[64,10,1,128]{3,0,2,1:T(8,128)S(1)} %get-tuple-element.113), channel_id=1, source_target_pairs={{0,1},{1,2},{2,3},{3,4},{4,5},{5,6},{6,7},{8,9},{9,10},{10,11},{11... | collective-permute-start | bytes 983048 | tf_op jit(solution)/shard_map/ppermute | solution.py:16
  125.7 1.9 collective-permute-start.15
  127.6 2.1 collective-permute-done.14
  129.7 4.4 collective-permute-done.15
  134.1 7.9 %multiply_divide_fusion = (f32[64,8,16,128]{3,0,2,1:T(8,128)S(1)}, f32[64,8,16,128]{3,0,2,1:T(8,128)S(1)}) fusion(f32[8,16,128]{2,1,0:T(8,128)S(1)} %get-tuple-element.100, f32[8,16,128]{2,1,0:T(8,128)S(1)} %get-tuple-element.106, f32[64,8,16,128]{3,0,2,1:T(8,128)S(1)} %fusion.18, f32[8,16,128]{2,1,0:T(8,128)S(1)} %get-tuple-element.105, ...), kind=kLoop, calls=%fused_computation.158 | loop fusion | flops 30408704 | bytes 16973824 | tf_op jit(solution)/shard_map/div | solution.py:45
  142.1 2.1 collective-permute-start.16
  145.5 6.0 %collective-permute-done.16 = f32[64,1,16,128]{3,0,2,1:T(8,128)S(1)} collective-permute-done((f32[64,1,16,128]{3,0,2,1:T(8,128)S(1)}, f32[64,1,16,128]{3,0,2,1:T(8,128)S(1)}, u32[]{:S(2)}, u32[]{:S(2)}) %collective-permute-start.16) | collective-permute-done | bytes 524320 | tf_op jit(solution)/shard_map/ppermute | solution.py:16
  151.5 4.1 collective-permute-done.17
  155.7 7.3 %collective-permute-start.18 = (f32[64,10,1,128]{3,0,2,1:T(8,128)S(1)}, f32[64,10,1,128]{3,0,2,1:T(8,128)S(1)}, u32[]{:S(2)}, u32[]{:S(2)}) collective-permute-start(f32[64,10,1,128]{3,0,2,1:T(8,128)S(1)} %get-tuple-element.111), channel_id=1, source_target_pairs={{0,1},{1,2},{2,3},{3,4},{4,5},{5,6},{6,7},{8,9},{9,10},{10,11},{11... | collective-permute-start | bytes 983048 | tf_op jit(solution)/shard_map/ppermute | solution.py:16
  163.0 2.4 collective-permute-start.19
  165.4 1.6 collective-permute-done.18
  167.0 4.4 collective-permute-done.19
  171.4 13.2 %fusion.34 = f32[64,8,16,128]{3,0,2,1:T(8,128)S(1)} fusion(f32[64,8,16,128]{3,0,2,1:T(8,128)S(1)} %get-tuple-element.99, f32[64,8,16,128]{3,0,2,1:T(8,128)} %copy-done.4, f32[64,10,1,128]{3,0,2,1:T(8,128)S(1)} %collective-permute-done.19, f32[64,1,16,128]{3,0,2,1:T(8,128)S(1)} %collective-permute-done.17, f32[64,1,16,128]{3,0,2,1:T(8,128)S(1)} %collective-permute-done.16, ...), kind=kLoop, calls=%fused_computation.47 | loop fusion | flops 25165824 | bytes 14745600 | tf_op jit(solution)/shard_map/add | solution.py:41
  184.7 1.3 collective-permute-start.20
  187.3 5.9 %collective-permute-done.20 = f32[64,1,16,128]{3,0,2,1:T(8,128)S(1)} collective-permute-done((f32[64,1,16,128]{3,0,2,1:T(8,128)S(1)}, f32[64,1,16,128]{3,0,2,1:T(8,128)S(1)}, u32[]{:S(2)}, u32[]{:S(2)}) %collective-permute-start.20) | collective-permute-done | bytes 524320 | tf_op jit(solution)/shard_map/ppermute | solution.py:16
  193.2 4.1 collective-permute-done.21
  197.4 6.9 %collective-permute-start.22 = (f32[64,10,1,128]{3,0,2,1:T(8,128)S(1)}, f32[64,10,1,128]{3,0,2,1:T(8,128)S(1)}, u32[]{:S(2)}, u32[]{:S(2)}) collective-permute-start(f32[64,10,1,128]{3,0,2,1:T(8,128)S(1)} %get-tuple-element.109), channel_id=1, source_target_pairs={{0,1},{1,2},{2,3},{3,4},{4,5},{5,6},{6,7},{8,9},{9,10},{10,11},{11... | collective-permute-start | bytes 983048 | tf_op jit(solution)/shard_map/ppermute | solution.py:16
  204.3 1.9 collective-permute-start.23
  206.3 2.1 collective-permute-done.22
  208.3 4.4 collective-permute-done.23
  212.7 13.2 %fusion.42 = f32[64,8,16,128]{3,0,2,1:T(8,128)S(1)} fusion(f32[64,8,16,128]{3,0,2,1:T(8,128)S(1)} %get-tuple-element.99, f32[64,8,16,128]{3,0,2,1:T(8,128)} %copy-done.3, f32[64,10,1,128]{3,0,2,1:T(8,128)S(1)} %collective-permute-done.23, f32[64,1,16,128]{3,0,2,1:T(8,128)S(1)} %collective-permute-done.21, f32[64,1,16,128]{3,0,2,1:T(8,128)S(1)} %collective-permute-done.20, ...), kind=kLoop, calls=%fused_computation.55 | loop fusion | flops 25165824 | bytes 14745600 | tf_op jit(solution)/shard_map/add | solution.py:41
  226.0 3.5 collective-permute-start.24
  230.8 6.0 %collective-permute-done.24 = f32[64,1,16,128]{3,0,2,1:T(8,128)S(1)} collective-permute-done((f32[64,1,16,128]{3,0,2,1:T(8,128)S(1)}, f32[64,1,16,128]{3,0,2,1:T(8,128)S(1)}, u32[]{:S(2)}, u32[]{:S(2)}) %collective-permute-start.24) | collective-permute-done | bytes 524320 | tf_op jit(solution)/shard_map/ppermute | solution.py:16
  236.8 4.1 collective-permute-done.25
  241.0 6.0 %collective-permute-start.26 = (f32[64,10,1,128]{3,0,2,1:T(8,128)S(1)}, f32[64,10,1,128]{3,0,2,1:T(8,128)S(1)}, u32[]{:S(2)}, u32[]{:S(2)}) collective-permute-start(f32[64,10,1,128]{3,0,2,1:T(8,128)S(1)} %get-tuple-element.107), channel_id=1, source_target_pairs={{0,1},{1,2},{2,3},{3,4},{4,5},{5,6},{6,7},{8,9},{9,10},{10,11},{11... | collective-permute-start | bytes 983048 | tf_op jit(solution)/shard_map/ppermute | solution.py:16
  247.0 2.1 collective-permute-start.27
  249.2 1.9 collective-permute-done.26
  251.0 4.4 collective-permute-done.27
  255.4 14.5 %fusion.97 = f32[64,8,16,128]{3,0,2,1:T(8,128)S(1)} fusion(f32[64,8,16,128]{3,0,2,1:T(8,128)} %copy-done, f32[64,8,16,128]{3,0,2,1:T(8,128)} %copy-done.2, f32[64,10,1,128]{3,0,2,1:T(8,128)S(1)} %collective-permute-done.27, f32[64,1,16,128]{3,0,2,1:T(8,128)S(1)} %collective-permute-done.25, f32[64,1,16,128]{3,0,2,1:T(8,128)S(1)} %collective-permute-done.24, ...), kind=kLoop, calls=%fused_computation.162 | loop fusion | flops 26214400 | bytes 14811136 | tf_op jit(solution)/shard_map/mul | solution.py:77
  269.9 2.0 copy-done.1
  271.9 3.4 fusion.98
  275.3 80.6 %psum.7 = f32[64,64]{0,1:T(8,128)S(1)} all-reduce(f32[64,64]{0,1:T(8,128)S(1)} %fusion.98), channel_id=1, replica_groups=mesh['gx'=32,'gy'=8] {'gx','gy'}, use_global_device_ids=true, to_apply=%region_0.1 | all-reduce | flops 4096 | bytes 32768 | tf_op jit(solution)/shard_map/psum | solution.py:81
  356.0 5.8 %cholesky.19 = f32[64,64]{1,0:T(8,128)S(1)} custom-call(f32[64,64]{1,0:T(8,128)S(1)} %fusion.112), custom_call_target="Cholesky" | custom-call | tf_op jit(solution)/shard_map/jit(cholesky)/cholesky | solution.py:82
  363.9 6.6 %copy.29 = f32[64,8,16,128]{3,2,1,0:T(8,128)} copy(f32[64,8,16,128]{3,0,2,1:T(8,128)} %copy-done.1) | data formatting | bytes 8388608 | tf_op jit(solution)/shard_map/mul | solution.py:77
  371.2 90.6 %while.13 = (s32[]{:T(128)}, f32[64,64]{1,0:T(8,128)S(1)}, f32[64,64]{1,0:T(8,128)S(1)}, f32[64,64]{1,0:T(8,128)S(1)}, s32[]{:T(128)}, /*index=5*/s32[]{:T(128)}) while((s32[]{:T(128)}, f32[64,64]{1,0:T(8,128)S(1)}, f32[64,64]{1,0:T(8,128)S(1)}, f32[64,64]{1,0:T(8,128)S(1)}, s32[]{:T(128)}, /*index=5*/s32[]{:T(128)}) %tuple.57), condition=%wide.region_4.5_spmd, body=%wide.region_3.4_spmd.sunk | while | flops 49282 | bytes 36181 | solution.py:66
  461.7 4.6 copy.46
  467.1 6.0 %fusion.94 = f32[64,8,16,128]{3,0,2,1:T(8,128)S(1)} fusion(f32[8,16,128,64]{2,1,0,3:T(8,128)S(1)} %bitcast.44, f32[64,64]{1,0:T(8,128)S(1)} %get-tuple-element.81), kind=kOutput, calls=%fused_computation.156 | convolution fusion | flops 805306368 | bytes 8404992 | tf_op jit(solution)/shard_map/dot_general | solution.py:84
  473.0 4.4 copy.31
  (243 shorter events, 104.1 us)
Async XLA Ops:
  1.3 5.7 %collective-permute-start = (f32[1,16,128]{2,1,0:T(8,128)S(1)}, f32[1,16,128]{2,1,0:T(8,128)S(1)}, u32[]{:S(2)}, u32[]{:S(2)}) collective-permute-start(f32[1,16,128]{2,1,0:T(8,128)S(1)} %get-tuple-element.134), channel_id=1, source_target_pairs={{0,8},{8,16},{16,24},{24,32},{32,40},{40,48},{48,56},{56,64},{64,7... | collective-permute-start | bytes 24584 | tf_op jit(solution)/shard_map/ppermute | solution.py:16
  5.7 4.6 collective-permute-start.1
  10.3 6.9 %collective-permute-start.2 = (f32[10,1,128]{2,1,0:T(1,128)S(1)}, f32[10,1,128]{2,1,0:T(1,128)S(1)}, u32[]{:S(2)}, u32[]{:S(2)}) collective-permute-start(f32[10,1,128]{2,1,0:T(1,128)S(1)} %get-tuple-element.132), channel_id=1, source_target_pairs={{0,1},{1,2},{2,3},{3,4},{4,5},{5,6},{6,7},{8,9},{9,10},{10,11},{11... | collective-permute-start | bytes 15368 | tf_op jit(solution)/shard_map/ppermute | solution.py:16
  15.3 4.9 %collective-permute-start.3 = (f32[10,1,128]{2,1,0:T(1,128)S(1)}, f32[10,1,128]{2,1,0:T(1,128)S(1)}, u32[]{:S(2)}, u32[]{:S(2)}) collective-permute-start(f32[10,1,128]{2,1,0:T(1,128)S(1)} %get-tuple-element.131), channel_id=1, source_target_pairs={{1,0},{2,1},{3,2},{4,3},{5,4},{6,5},{7,6},{9,8},{10,9},{11,10},{12... | collective-permute-start | bytes 15368 | tf_op jit(solution)/shard_map/ppermute | solution.py:17
  24.8 31.6 %copy-start.5 = (bf16[64,8,16,128]{3,2,1,0:T(8,128)(2,1)S(1)}, bf16[64,8,16,128]{3,2,1,0:T(8,128)(2,1)}, u32[]{:S(2)}) copy-start(bf16[64,8,16,128]{3,2,1,0:T(8,128)(2,1)} %param.7) | copy-start | bytes 6291460
  24.8 31.6 %copy-start.6 = (f32[8,16,128]{2,1,0:T(8,128)S(1)}, f32[8,16,128]{2,1,0:T(8,128)}, u32[]{:S(2)}) copy-start(f32[8,16,128]{2,1,0:T(8,128)} %param.10) | copy-start | bytes 196612
  24.9 14.0 %collective-permute-start.4 = (f32[64,1,16,128]{3,0,2,1:T(8,128)S(1)}, f32[64,1,16,128]{3,0,2,1:T(8,128)S(1)}, u32[]{:S(2)}, u32[]{:S(2)}) collective-permute-start(f32[64,1,16,128]{3,0,2,1:T(8,128)S(1)} %get-tuple-element.129), channel_id=1, source_target_pairs={{0,8},{8,16},{16,24},{24,32},{32,40},{40,48},{48,56},{56,64},{64,7... | collective-permute-start | bytes 1572872 | tf_op jit(solution)/shard_map/ppermute | solution.py:16
  28.6 15.4 %collective-permute-start.5 = (f32[64,1,16,128]{3,0,2,1:T(8,128)S(1)}, f32[64,1,16,128]{3,0,2,1:T(8,128)S(1)}, u32[]{:S(2)}, u32[]{:S(2)}) collective-permute-start(f32[64,1,16,128]{3,0,2,1:T(8,128)S(1)} %get-tuple-element.130), channel_id=1, source_target_pairs={{8,0},{16,8},{24,16},{32,24},{40,32},{48,40},{56,48},{64,56},{72,6... | collective-permute-start | bytes 1572872 | tf_op jit(solution)/shard_map/ppermute | solution.py:17
  44.1 7.9 %collective-permute-start.6 = (f32[64,10,1,128]{3,0,2,1:T(8,128)S(1)}, f32[64,10,1,128]{3,0,2,1:T(8,128)S(1)}, u32[]{:S(2)}, u32[]{:S(2)}) collective-permute-start(f32[64,10,1,128]{3,0,2,1:T(8,128)S(1)} %get-tuple-element.117), channel_id=1, source_target_pairs={{0,1},{1,2},{2,3},{3,4},{4,5},{5,6},{6,7},{8,9},{9,10},{10,11},{11... | collective-permute-start | bytes 983048 | tf_op jit(solution)/shard_map/ppermute | solution.py:16
  48.0 8.4 %collective-permute-start.7 = (f32[64,10,1,128]{3,0,2,1:T(8,128)S(1)}, f32[64,10,1,128]{3,0,2,1:T(8,128)S(1)}, u32[]{:S(2)}, u32[]{:S(2)}) collective-permute-start(f32[64,10,1,128]{3,0,2,1:T(8,128)S(1)} %get-tuple-element.118), channel_id=1, source_target_pairs={{1,0},{2,1},{3,2},{4,3},{5,4},{6,5},{7,6},{9,8},{10,9},{11,10},{12... | collective-permute-start | bytes 983048 | tf_op jit(solution)/shard_map/ppermute | solution.py:17
  64.3 12.2 %collective-permute-start.8 = (f32[64,1,16,128]{3,0,2,1:T(8,128)S(1)}, f32[64,1,16,128]{3,0,2,1:T(8,128)S(1)}, u32[]{:S(2)}, u32[]{:S(2)}) collective-permute-start(f32[64,1,16,128]{3,0,2,1:T(8,128)S(1)} %get-tuple-element.127), channel_id=1, source_target_pairs={{0,8},{8,16},{16,24},{24,32},{32,40},{40,48},{48,56},{56,64},{64,7... | collective-permute-start | bytes 1572872 | tf_op jit(solution)/shard_map/ppermute | solution.py:16
  69.2 11.7 %collective-permute-start.9 = (f32[64,1,16,128]{3,0,2,1:T(8,128)S(1)}, f32[64,1,16,128]{3,0,2,1:T(8,128)S(1)}, u32[]{:S(2)}, u32[]{:S(2)}) collective-permute-start(f32[64,1,16,128]{3,0,2,1:T(8,128)S(1)} %get-tuple-element.128), channel_id=1, source_target_pairs={{8,0},{16,8},{24,16},{32,24},{40,32},{48,40},{56,48},{64,56},{72,6... | collective-permute-start | bytes 1572872 | tf_op jit(solution)/shard_map/ppermute | solution.py:17
  81.0 10.2 %collective-permute-start.10 = (f32[64,10,1,128]{3,0,2,1:T(8,128)S(1)}, f32[64,10,1,128]{3,0,2,1:T(8,128)S(1)}, u32[]{:S(2)}, u32[]{:S(2)}) collective-permute-start(f32[64,10,1,128]{3,0,2,1:T(8,128)S(1)} %get-tuple-element.115), channel_id=1, source_target_pairs={{0,1},{1,2},{2,3},{3,4},{4,5},{5,6},{6,7},{8,9},{9,10},{10,11},{11... | collective-permute-start | bytes 983048 | tf_op jit(solution)/shard_map/ppermute | solution.py:16
  87.2 8.4 %collective-permute-start.11 = (f32[64,10,1,128]{3,0,2,1:T(8,128)S(1)}, f32[64,10,1,128]{3,0,2,1:T(8,128)S(1)}, u32[]{:S(2)}, u32[]{:S(2)}) collective-permute-start(f32[64,10,1,128]{3,0,2,1:T(8,128)S(1)} %get-tuple-element.116), channel_id=1, source_target_pairs={{1,0},{2,1},{3,2},{4,3},{5,4},{6,5},{7,6},{9,8},{10,9},{11,10},{12... | collective-permute-start | bytes 983048 | tf_op jit(solution)/shard_map/ppermute | solution.py:17
  103.4 30.7 %copy-start.7 = (f32[8,16,128]{2,1,0:T(8,128)S(1)}, f32[8,16,128]{2,1,0:T(8,128)}, u32[]{:S(2)}) copy-start(f32[8,16,128]{2,1,0:T(8,128)} %param.11) | copy-start | bytes 196612
  103.5 11.3 %collective-permute-start.12 = (f32[64,1,16,128]{3,0,2,1:T(8,128)S(1)}, f32[64,1,16,128]{3,0,2,1:T(8,128)S(1)}, u32[]{:S(2)}, u32[]{:S(2)}) collective-permute-start(f32[64,1,16,128]{3,0,2,1:T(8,128)S(1)} %get-tuple-element.125), channel_id=1, source_target_pairs={{0,8},{8,16},{16,24},{24,32},{32,40},{40,48},{48,56},{56,64},{64,7... | collective-permute-start | bytes 1572872 | tf_op jit(solution)/shard_map/ppermute | solution.py:16
  107.5 11.4 %collective-permute-start.13 = (f32[64,1,16,128]{3,0,2,1:T(8,128)S(1)}, f32[64,1,16,128]{3,0,2,1:T(8,128)S(1)}, u32[]{:S(2)}, u32[]{:S(2)}) collective-permute-start(f32[64,1,16,128]{3,0,2,1:T(8,128)S(1)} %get-tuple-element.126), channel_id=1, source_target_pairs={{8,0},{16,8},{24,16},{32,24},{40,32},{48,40},{56,48},{64,56},{72,6... | collective-permute-start | bytes 1572872 | tf_op jit(solution)/shard_map/ppermute | solution.py:17
  119.0 10.7 %collective-permute-start.14 = (f32[64,10,1,128]{3,0,2,1:T(8,128)S(1)}, f32[64,10,1,128]{3,0,2,1:T(8,128)S(1)}, u32[]{:S(2)}, u32[]{:S(2)}) collective-permute-start(f32[64,10,1,128]{3,0,2,1:T(8,128)S(1)} %get-tuple-element.113), channel_id=1, source_target_pairs={{0,1},{1,2},{2,3},{3,4},{4,5},{5,6},{6,7},{8,9},{9,10},{10,11},{11... | collective-permute-start | bytes 983048 | tf_op jit(solution)/shard_map/ppermute | solution.py:16
  125.7 8.4 %collective-permute-start.15 = (f32[64,10,1,128]{3,0,2,1:T(8,128)S(1)}, f32[64,10,1,128]{3,0,2,1:T(8,128)S(1)}, u32[]{:S(2)}, u32[]{:S(2)}) collective-permute-start(f32[64,10,1,128]{3,0,2,1:T(8,128)S(1)} %get-tuple-element.114), channel_id=1, source_target_pairs={{1,0},{2,1},{3,2},{4,3},{5,4},{6,5},{7,6},{9,8},{10,9},{11,10},{12... | collective-permute-start | bytes 983048 | tf_op jit(solution)/shard_map/ppermute | solution.py:17
  142.0 29.3 %copy-start.4 = (f32[64,8,16,128]{3,0,2,1:T(8,128)}, f32[64,8,16,128]{3,0,2,1:T(8,128)S(1)}, u32[]{:S(2)}) copy-start(f32[64,8,16,128]{3,0,2,1:T(8,128)S(1)} %get-tuple-element.98) | copy-start | bytes 12582916
  142.1 70.7 %copy-start = (f32[64,8,16,128]{3,0,2,1:T(8,128)}, f32[64,8,16,128]{3,0,2,1:T(8,128)S(1)}, u32[]{:S(2)}) copy-start(f32[64,8,16,128]{3,0,2,1:T(8,128)S(1)} %get-tuple-element.99) | copy-start | bytes 12582916
  142.1 9.4 %collective-permute-start.16 = (f32[64,1,16,128]{3,0,2,1:T(8,128)S(1)}, f32[64,1,16,128]{3,0,2,1:T(8,128)S(1)}, u32[]{:S(2)}, u32[]{:S(2)}) collective-permute-start(f32[64,1,16,128]{3,0,2,1:T(8,128)S(1)} %get-tuple-element.123), channel_id=1, source_target_pairs={{0,8},{8,16},{16,24},{24,32},{32,40},{40,48},{48,56},{56,64},{64,7... | collective-permute-start | bytes 1572872 | tf_op jit(solution)/shard_map/ppermute | solution.py:16
  144.2 11.4 %collective-permute-start.17 = (f32[64,1,16,128]{3,0,2,1:T(8,128)S(1)}, f32[64,1,16,128]{3,0,2,1:T(8,128)S(1)}, u32[]{:S(2)}, u32[]{:S(2)}) collective-permute-start(f32[64,1,16,128]{3,0,2,1:T(8,128)S(1)} %get-tuple-element.124), channel_id=1, source_target_pairs={{8,0},{16,8},{24,16},{32,24},{40,32},{48,40},{56,48},{64,56},{72,6... | collective-permute-start | bytes 1572872 | tf_op jit(solution)/shard_map/ppermute | solution.py:17
  155.7 11.3 %collective-permute-start.18 = (f32[64,10,1,128]{3,0,2,1:T(8,128)S(1)}, f32[64,10,1,128]{3,0,2,1:T(8,128)S(1)}, u32[]{:S(2)}, u32[]{:S(2)}) collective-permute-start(f32[64,10,1,128]{3,0,2,1:T(8,128)S(1)} %get-tuple-element.111), channel_id=1, source_target_pairs={{0,1},{1,2},{2,3},{3,4},{4,5},{5,6},{6,7},{8,9},{9,10},{10,11},{11... | collective-permute-start | bytes 983048 | tf_op jit(solution)/shard_map/ppermute | solution.py:16
  163.0 8.4 %collective-permute-start.19 = (f32[64,10,1,128]{3,0,2,1:T(8,128)S(1)}, f32[64,10,1,128]{3,0,2,1:T(8,128)S(1)}, u32[]{:S(2)}, u32[]{:S(2)}) collective-permute-start(f32[64,10,1,128]{3,0,2,1:T(8,128)S(1)} %get-tuple-element.112), channel_id=1, source_target_pairs={{1,0},{2,1},{3,2},{4,3},{5,4},{6,5},{7,6},{9,8},{10,9},{11,10},{12... | collective-permute-start | bytes 983048 | tf_op jit(solution)/shard_map/ppermute | solution.py:17
  184.6 23.7 %copy-start.3 = (f32[64,8,16,128]{3,0,2,1:T(8,128)}, f32[64,8,16,128]{3,0,2,1:T(8,128)S(1)}, u32[]{:S(2)}) copy-start(f32[64,8,16,128]{3,0,2,1:T(8,128)S(1)} %fusion.34) | copy-start | bytes 12582916
  184.7 8.5 %collective-permute-start.20 = (f32[64,1,16,128]{3,0,2,1:T(8,128)S(1)}, f32[64,1,16,128]{3,0,2,1:T(8,128)S(1)}, u32[]{:S(2)}, u32[]{:S(2)}) collective-permute-start(f32[64,1,16,128]{3,0,2,1:T(8,128)S(1)} %get-tuple-element.121), channel_id=1, source_target_pairs={{0,8},{8,16},{16,24},{24,32},{32,40},{40,48},{48,56},{56,64},{64,7... | collective-permute-start | bytes 1572872 | tf_op jit(solution)/shard_map/ppermute | solution.py:16
  186.0 11.3 %collective-permute-start.21 = (f32[64,1,16,128]{3,0,2,1:T(8,128)S(1)}, f32[64,1,16,128]{3,0,2,1:T(8,128)S(1)}, u32[]{:S(2)}, u32[]{:S(2)}) collective-permute-start(f32[64,1,16,128]{3,0,2,1:T(8,128)S(1)} %get-tuple-element.122), channel_id=1, source_target_pairs={{8,0},{16,8},{24,16},{32,24},{40,32},{48,40},{56,48},{64,56},{72,6... | collective-permute-start | bytes 1572872 | tf_op jit(solution)/shard_map/ppermute | solution.py:17
  197.4 10.9 %collective-permute-start.22 = (f32[64,10,1,128]{3,0,2,1:T(8,128)S(1)}, f32[64,10,1,128]{3,0,2,1:T(8,128)S(1)}, u32[]{:S(2)}, u32[]{:S(2)}) collective-permute-start(f32[64,10,1,128]{3,0,2,1:T(8,128)S(1)} %get-tuple-element.109), channel_id=1, source_target_pairs={{0,1},{1,2},{2,3},{3,4},{4,5},{5,6},{6,7},{8,9},{9,10},{10,11},{11... | collective-permute-start | bytes 983048 | tf_op jit(solution)/shard_map/ppermute | solution.py:16
  204.3 8.4 %collective-permute-start.23 = (f32[64,10,1,128]{3,0,2,1:T(8,128)S(1)}, f32[64,10,1,128]{3,0,2,1:T(8,128)S(1)}, u32[]{:S(2)}, u32[]{:S(2)}) collective-permute-start(f32[64,10,1,128]{3,0,2,1:T(8,128)S(1)} %get-tuple-element.110), channel_id=1, source_target_pairs={{1,0},{2,1},{3,2},{4,3},{5,4},{6,5},{7,6},{9,8},{10,9},{11,10},{12... | collective-permute-start | bytes 983048 | tf_op jit(solution)/shard_map/ppermute | solution.py:17
  225.9 15.0 %copy-start.2 = (f32[64,8,16,128]{3,0,2,1:T(8,128)}, f32[64,8,16,128]{3,0,2,1:T(8,128)S(1)}, u32[]{:S(2)}) copy-start(f32[64,8,16,128]{3,0,2,1:T(8,128)S(1)} %fusion.42) | copy-start | bytes 12582916
  226.0 10.8 %collective-permute-start.24 = (f32[64,1,16,128]{3,0,2,1:T(8,128)S(1)}, f32[64,1,16,128]{3,0,2,1:T(8,128)S(1)}, u32[]{:S(2)}, u32[]{:S(2)}) collective-permute-start(f32[64,1,16,128]{3,0,2,1:T(8,128)S(1)} %get-tuple-element.119), channel_id=1, source_target_pairs={{0,8},{8,16},{16,24},{24,32},{32,40},{40,48},{48,56},{56,64},{64,7... | collective-permute-start | bytes 1572872 | tf_op jit(solution)/shard_map/ppermute | solution.py:16
  229.5 11.4 %collective-permute-start.25 = (f32[64,1,16,128]{3,0,2,1:T(8,128)S(1)}, f32[64,1,16,128]{3,0,2,1:T(8,128)S(1)}, u32[]{:S(2)}, u32[]{:S(2)}) collective-permute-start(f32[64,1,16,128]{3,0,2,1:T(8,128)S(1)} %get-tuple-element.120), channel_id=1, source_target_pairs={{8,0},{16,8},{24,16},{32,24},{40,32},{48,40},{56,48},{64,56},{72,6... | collective-permute-start | bytes 1572872 | tf_op jit(solution)/shard_map/ppermute | solution.py:17
  241.0 10.0 %collective-permute-start.26 = (f32[64,10,1,128]{3,0,2,1:T(8,128)S(1)}, f32[64,10,1,128]{3,0,2,1:T(8,128)S(1)}, u32[]{:S(2)}, u32[]{:S(2)}) collective-permute-start(f32[64,10,1,128]{3,0,2,1:T(8,128)S(1)} %get-tuple-element.107), channel_id=1, source_target_pairs={{0,1},{1,2},{2,3},{3,4},{4,5},{5,6},{6,7},{8,9},{9,10},{10,11},{11... | collective-permute-start | bytes 983048 | tf_op jit(solution)/shard_map/ppermute | solution.py:16
  247.0 8.4 %collective-permute-start.27 = (f32[64,10,1,128]{3,0,2,1:T(8,128)S(1)}, f32[64,10,1,128]{3,0,2,1:T(8,128)S(1)}, u32[]{:S(2)}, u32[]{:S(2)}) collective-permute-start(f32[64,10,1,128]{3,0,2,1:T(8,128)S(1)} %get-tuple-element.108), channel_id=1, source_target_pairs={{1,0},{2,1},{3,2},{4,3},{5,4},{6,5},{7,6},{9,8},{10,9},{11,10},{12... | collective-permute-start | bytes 983048 | tf_op jit(solution)/shard_map/ppermute | solution.py:17
  269.9 2.0 copy-start.1
where the time goes:
time: 487 us; the launch traced here: 478 us
  waiting for transfers between devices  108 us (22%)
  starting transfers between devices  88.9 us (18%)
  blocking collectives  80.6 us (17%)
  other arithmetic  77.1 us (16%)
  local copies, waits for them, and re-layouts  60.6 us (12%)
  matrix products  59.3 us (12%)
    psum x1, blocking collectives, body(): summed = lax.psum(gram, ('gx', 'gy'))  80.6 us
    ppermute x14, starting transfers between devices, padded_2(): before = lax.ppermute(last, axis, up)  65.8 us
    ppermute x14, waiting for transfers between devices, padded_2(): after = lax.ppermute(first, axis, down)  57.8 us
    ppermute x14, waiting for transfers between devices, padded_2(): before = lax.ppermute(last, axis, up)  50.6 us
    dot_general x64, matrix products, row_step(): jnp.dot(row, inverse, precision=lax.Precision.HIGHEST, preferred_element_...  50 us
    add x4, other arithmetic, sweep(): return 0.2 * field + 0.8 * (rhs + total) / diag  42 us
    dynamic_slice x64, local copies, waits for them, and re-layouts, row_step(): pivot = lax.dynamic_slice(lower, (index, index), (1, 1))  37.6 us
    ppermute x14, starting transfers between devices, padded_2(): after = lax.ppermute(first, axis, down)  23.1 us
  transfers between devices with their start and end apart: 28, of which 26 were waited for; matrix products, arithmetic and copies ran while one was open for 0% of the time, Pallas kernels for 0%

commit v1 on v0

v1 whole, which is shorter than its diff:
```python
import functools

import jax
import jax.numpy as jnp
from jax import lax
from jax.experimental import pallas as pl
from jax.experimental.pallas import tpu as pltpu
from jax.sharding import PartitionSpec as P

MESH = pl.DeviceIdType.MESH
GROUPS = 4
ROWS = 4
XLO, XHI, YLO, YHI = range(4)


def remote(src, dst, send, recv, where):
    return pltpu.make_async_remote_copy(
        src_ref=src, dst_ref=dst, send_sem=send, recv_sem=recv, device_id=where, device_id_type=MESH
    )


def respond_kernel(
    dims,
    probes, perm, absorption, sensitivity, weight,
    y_out, gram_out,
    field, rhs, stage, kpad, kface, khalo_x, khalo_y, natural, spread,
    slot_c, slot_y, slot_x, slot_z,
    k_send, k_recv, f_send, f_recv, r_send, r_recv,
):
    peers_x, peers_y, chips_x, chips_y, chips_z = dims
    count, wx, wy, wz = probes.shape
    size = count // GROUPS
    tiles = size // 8
    gx, gy = lax.axis_index("gx"), lax.axis_index("gy")
    cx, cz = gx // chips_z, gx % chips_z
    cy, core = gy // 2, gy % 2

    x_before = ((gx + peers_x - 1) % peers_x, gy)
    x_after = ((gx + 1) % peers_x, gy)
    y_before = (gx, (gy + peers_y - 1) % peers_y)
    y_after = (gx, (gy + 1) % peers_y)
    other_core = [(gx, cy * 2 + 1 - core)]
    other_y = [(gx, (cy + j) % chips_y * 2 + core) for j in range(1, chips_y)]
    other_x = [((cx + j) % chips_x * chips_z + cz, gy) for j in range(1, chips_x)]
    other_z = [(cx * chips_z + (cz + j) % chips_z, gy) for j in range(1, chips_z)]

    barrier = pltpu.get_barrier_semaphore()
    everyone = [x_before, x_after, y_before, y_after] + other_core + other_y + other_x + other_z
    for where in everyone:
        pl.semaphore_signal(barrier, inc=1, device_id=where, device_id_type=MESH)
    pl.semaphore_wait(barrier, len(everyone))

    kface[0] = perm[:, 0, :]
    kface[1] = perm[:, wy - 1, :]
    k_copies = [
        remote(perm.at[wx - 1], khalo_x.at[0], k_send.at[0], k_recv.at[0], x_after),
        remote(perm.at[0], khalo_x.at[1], k_send.at[1], k_recv.at[1], x_before),
        remote(kface.at[1], khalo_y.at[0], k_send.at[2], k_recv.at[2], y_after),
        remote(kface.at[0], khalo_y.at[1], k_send.at[3], k_recv.at[3], y_before),
    ]
    for copy in k_copies:
        copy.start()
    for copy in k_copies:
        copy.wait()

    has_x_low = jnp.where(gx > 0, 1.0, 0.0).astype(jnp.float32)
    has_x_high = jnp.where(gx < peers_x - 1, 1.0, 0.0).astype(jnp.float32)
    has_y_low = jnp.where(gy > 0, 1.0, 0.0).astype(jnp.float32)
    has_y_high = jnp.where(gy < peers_y - 1, 1.0, 0.0).astype(jnp.float32)

    center = perm[...]
    kpad[pl.ds(1, wx), pl.ds(8, wy), :] = center
    kpad[0, pl.ds(8, wy), :] = khalo_x[0] * has_x_low
    kpad[wx + 1, pl.ds(8, wy), :] = khalo_x[1] * has_x_high
    for x in range(wx):
        kpad[x + 1, 7:8, :] = khalo_y[0, x:x + 1, :] * has_y_low
        kpad[x + 1, wy + 8:wy + 9, :] = khalo_y[1, x:x + 1, :] * has_y_high
    lane = lax.broadcasted_iota(jnp.int32, (wx, wy, wz), 2)
    x_at = lax.broadcasted_iota(jnp.int32, (wx, wy, wz), 0)
    y_at = lax.broadcasted_iota(jnp.int32, (wx, wy, wz), 1)

    def turned(value, shift):
        flat = pltpu.roll(value.reshape(-1, wz), shift, 1)
        return flat.reshape(value.shape)

    x_low = 0.5 * (center + kpad[pl.ds(0, wx), pl.ds(8, wy), :])
    x_high = 0.5 * (center + kpad[pl.ds(2, wx), pl.ds(8, wy), :])
    y_low = 0.5 * (center + kpad[pl.ds(1, wx), pl.ds(7, wy), :])
    y_high = 0.5 * (center + kpad[pl.ds(1, wx), pl.ds(9, wy), :])
    z_low = 0.5 * (center + jnp.where(lane == 0, 0.0, turned(center, 1)))
    z_high = 0.5 * (center + jnp.where(lane == wz - 1, 0.0, turned(center, wz - 1)))
    diag = absorption[...] + x_low + x_high + y_low + y_high + z_low + z_high
    damp = 0.8 / diag
    natural[0] = damp * jnp.where(x_at == 0, x_low * has_x_low, x_low)
    natural[1] = damp * jnp.where(x_at == wx - 1, x_high * has_x_high, x_high)
    natural[2] = damp * jnp.where(y_at == 0, y_low * has_y_low, y_low)
    natural[3] = damp * jnp.where(y_at == wy - 1, y_high * has_y_high, y_high)
    natural[4] = damp * jnp.where(lane == 0, 0.0, z_low)
    natural[5] = damp * jnp.where(lane == wz - 1, 0.0, z_high)
    natural[6] = damp * weight[...]
    natural[7] = sensitivity[...]
    natural[8] = damp * sensitivity[...]

    def faces(k, g):
        half = k % 2
        slot = half * GROUPS + g
        mine = field.at[slot]
        sides = (
            (mine.at[wx, pl.ds(1, wy)], mine.at[0, pl.ds(1, wy)], x_after),
            (mine.at[1, pl.ds(1, wy)], mine.at[wx + 1, pl.ds(1, wy)], x_before),
            (mine.at[pl.ds(1, wx), wy], mine.at[pl.ds(1, wx), 0], y_after),
            (mine.at[pl.ds(1, wx), 1], mine.at[pl.ds(1, wx), wy + 1], y_before),
        )
        return [
            remote(src, dst, f_send.at[slot, i], f_recv.at[slot, i], where)
            for i, (src, dst, where) in enumerate(sides)
        ]

    def first(g, carry):
        def plane(x, carry):
            def one(p, carry):
                value = probes[g * size + p, x].astype(jnp.float32) * natural[8, x]
                stage[pl.ds(p, wy, stride=size), :] = value
                return carry

            lax.fori_loop(0, size, one, 0, unroll=True)
            value = stage[...].reshape(wy, size, wz)
            field[g, x + 1, pl.ds(1, wy)] = value
            rhs[g, x] = value
            return carry

        lax.fori_loop(0, wx, plane, 0)
        for copy in faces(0, g):
            copy.start()
        return carry

    lax.fori_loop(0, GROUPS, first, 0)

    def widen(x, carry):
        for j in range(8):
            block = natural[j, x]
            for y in range(wy):
                spread[j, x, y] = jnp.broadcast_to(block[y:y + 1, :], (8, wz))
        return carry

    lax.fori_loop(0, wx, widen, 0)

    def sweep(k, g, last):
        old, new = (k % 2) * GROUPS + g, ((k + 1) % 2) * GROUPS + g

        def some(i, carry):
            x, y = i // (wy // ROWS), (i % (wy // ROWS)) * ROWS
            shape = (ROWS, tiles, 8, wz)

            def near(dx, dy):
                return field[old, x + 1 + dx, pl.ds(y + 1 + dy, ROWS)].reshape(shape)

            def factor(j):
                return spread[j, x, pl.ds(y, ROWS)].reshape(ROWS, 1, 8, wz)

            here = near(0, 0)
            total = rhs[g, x, pl.ds(y, ROWS)].reshape(shape) + 0.2 * here
            total = total + factor(0) * near(-1, 0) + factor(1) * near(1, 0)
            total = total + factor(2) * near(0, -1) + factor(3) * near(0, 1)
            total = total + factor(4) * turned(here, 1) + factor(5) * turned(here, wz - 1)
            if last == 2:
                total = total * factor(7)
                high = total.reshape(ROWS, size, wz).astype(jnp.bfloat16)
                low = (total.reshape(ROWS, size, wz) - high.astype(jnp.float32)).astype(jnp.bfloat16)
                at = pl.multiple_of(g * size, size)
                y_out[x, pl.ds(y, ROWS), pl.ds(at, size), :] = high
                y_out[x, pl.ds(y, ROWS), pl.ds(count + at, size), :] = low
                return carry
            if last == 1:
                total = total * factor(6)
                rhs[g, x, pl.ds(y, ROWS)] = total.reshape(ROWS, size, wz)
            field[new, x + 1, pl.ds(y + 1, ROWS)] = total.reshape(ROWS, size, wz)
            return carry

        lax.fori_loop(0, wx * wy // ROWS, some, 0)

    def step(k, g, first_of_all, last):
        if not first_of_all:
            for copy in faces(k + 1, g):
                copy.wait_send()
        for copy in faces(k, g):
            copy.wait_recv()
        sweep(k, g, last)
        if last != 2:
            for copy in faces(k + 1, g):
                copy.start()

    def run(k, g, first_of_all, last):
        def body(g, carry):
            step(k, g, first_of_all, last)
            return carry
        lax.fori_loop(0, GROUPS, body, 0)

    run(0, None, True, 0)
    run(1, None, False, 0)
    run(2, None, False, 1)

    def middle(i, carry):
        step(3 + i // GROUPS, i % GROUPS, False, 0)
        return carry
    lax.fori_loop(0, 2 * GROUPS, middle, 0)
    run(5, None, False, 2)

    def drain(g, carry):
        for copy in faces(5, g):
            copy.wait_send()
        return carry
    lax.fori_loop(0, GROUPS, drain, 0)

    def add(i, acc):
        x, y = i // (wy // 2), (i % (wy // 2)) * 2
        both = jnp.concatenate([y_out[x, y], y_out[x, y + 1]], axis=1)
        return acc + lax.dot_general(
            both, both, (((1,), (1,)), ((), ())), preferred_element_type=jnp.float32
        )

    product = lax.fori_loop(0, wx * wy // 2, add, jnp.zeros((2 * count, 2 * count), jnp.float32))
    folded = product[:count] + product[count:]
    folded = folded + pltpu.roll(folded, count, 1)
    half = count // 2
    lane2 = lax.broadcasted_iota(jnp.int32, (half, 2 * count), 1)
    packed = jnp.where(lane2 < count, folded[:half], folded[half:])

    base = 0
    for slots, me, others in (
        (slot_c, core, other_core), (slot_y, cy, other_y), (slot_x, cx, other_x), (slot_z, cz, other_z)
    ):
        n = len(others) + 1
        slots[me] = packed
        copies = [
            remote(slots.at[me], slots.at[me], r_send.at[base + j], r_recv.at[base + j], where)
            for j, where in enumerate(others)
        ]
        for copy in copies:
            copy.start()
        for copy in copies:
            copy.wait()
        packed = slots[0]
        for j in range(1, n):
            packed = packed + slots[j]
        base += n - 1
    cells = float(wx * peers_x * wy * peers_y * wz)
    gram_out[...] = packed / cells


def basis_kernel(y_ref, gram_ref, q_ref, r_ref, mix, stage):
    count = q_ref.shape[0]
    half = count // 2
    wy, wz = q_ref.shape[2], q_ref.shape[3]

    @pl.when(pl.program_id(0) == 0)
    def _():
        packed = gram_ref[...]
        rows = lax.broadcasted_iota(jnp.int32, (count, 2 * count), 0)
        lanes = lax.broadcasted_iota(jnp.int32, (count, 2 * count), 1)
        whole = jnp.concatenate([packed, pltpu.roll(packed, count, 1)], axis=0)
        work = jnp.where(lanes < count, whole, jnp.where(lanes - count == rows, 1.0, 0.0))
        scale = jnp.zeros((count, 1), jnp.float32)
        tall = lax.broadcasted_iota(jnp.int32, (count, 1), 0)
        for k in range(count):
            row = work[k:k + 1, :]
            pivot = row[:, k:k + 1]
            column = jnp.where(tall > k, work[:, k:k + 1], 0.0)
            scale = jnp.where(tall == k, pivot, scale)
            work = work - column * (row / pivot)
        work = work * lax.rsqrt(scale)
        r_ref[...] = jnp.where(lanes >= rows, work, 0.0)[:, :count]
        inverse = jnp.where(lanes < count, pltpu.roll(work, count, 1), work)
        high = inverse.astype(jnp.bfloat16)
        low = (inverse - high.astype(jnp.float32)).astype(jnp.bfloat16)
        mix[:, :2 * count] = high
        mix[:, 2 * count:] = low

    weights = mix[...]
    for y in range(0, wy, 2):
        both = jnp.concatenate([y_ref[0, y], y_ref[0, y + 1]], axis=1)
        both = jnp.concatenate([both, both], axis=0)
        out = jnp.dot(weights, both, preferred_element_type=jnp.float32)
        stage[pl.ds(y, count, stride=wy), :] = out[:, :wz]
        stage[pl.ds(y + 1, count, stride=wy), :] = out[:, wz:]
    q_ref[:, 0] = stage[...].reshape(count, wy, wz)


def body(dims, probes, permeability, absorption, sensitivity, observe_weight):
    count, wx, wy, wz = probes.shape
    size = count // GROUPS
    peers_x, peers_y, chips_x, chips_y, chips_z = dims
    f32 = jnp.float32
    vmem = pl.BlockSpec(memory_space=pltpu.VMEM)
    hops = 1 + chips_y - 1 + chips_x - 1 + chips_z - 1
    half = count // 2
    responses, gram = pl.pallas_call(
        functools.partial(respond_kernel, dims),
        out_shape=(
            jax.ShapeDtypeStruct((wx, wy, 2 * count, wz), jnp.bfloat16),
            jax.ShapeDtypeStruct((half, 2 * count), f32),
        ),
        in_specs=[vmem] * 5,
        out_specs=(vmem, vmem),
        scratch_shapes=[
            pltpu.VMEM((2 * GROUPS, wx + 2, wy + 2, size, wz), f32),
            pltpu.VMEM((GROUPS, wx, wy, size, wz), f32),
            pltpu.VMEM((wy * size, wz), f32),
            pltpu.VMEM((wx + 2, wy + 16, wz), f32),
            pltpu.VMEM((2, wx, wz), f32),
            pltpu.VMEM((2, wy, wz), f32),
            pltpu.VMEM((2, wx, wz), f32),
            pltpu.VMEM((9, wx, wy, wz), f32),
            pltpu.VMEM((8, wx, wy, 8, wz), f32),
            pltpu.VMEM((2, half, 2 * count), f32),
            pltpu.VMEM((chips_y, half, 2 * count), f32),
            pltpu.VMEM((chips_x, half, 2 * count), f32),
            pltpu.VMEM((chips_z, half, 2 * count), f32),
            pltpu.SemaphoreType.DMA((4,)),
            pltpu.SemaphoreType.DMA((4,)),
            pltpu.SemaphoreType.DMA((2 * GROUPS, 4)),
            pltpu.SemaphoreType.DMA((2 * GROUPS, 4)),
            pltpu.SemaphoreType.DMA((hops,)),
            pltpu.SemaphoreType.DMA((hops,)),
        ],
        compiler_params=pltpu.CompilerParams(
            collective_id=0, has_side_effects=True, vmem_limit_bytes=52 * 2**20
        ),
    )(probes, permeability, absorption, sensitivity, observe_weight)

    q_basis, r_factor = pl.pallas_call(
        basis_kernel,
        grid=(wx,),
        out_shape=(
            jax.ShapeDtypeStruct((count, wx, wy, wz), f32),
            jax.ShapeDtypeStruct((count, count), f32),
        ),
        in_specs=[
            pl.BlockSpec((1, wy, 2 * count, wz), lambda i: (i, 0, 0, 0)),
            pl.BlockSpec((half, 2 * count), lambda i: (0, 0)),
        ],
        out_specs=(
            pl.BlockSpec((count, 1, wy, wz), lambda i: (0, i, 0, 0)),
            pl.BlockSpec((count, count), lambda i: (0, 0)),
        ),
        scratch_shapes=[
            pltpu.VMEM((count, 4 * count), jnp.bfloat16),
            pltpu.VMEM((count * wy, wz), f32),
        ],
        compiler_params=pltpu.CompilerParams(vmem_limit_bytes=32 * 2**20),
    )(responses, gram)
    return q_basis, r_factor


def solution(mesh):
    peers_x, peers_y = mesh.shape["gx"], mesh.shape["gy"]
    chips_x = 4
    dims = (peers_x, peers_y, chips_x, peers_y // 2, peers_x // chips_x)
    cell = P("gx", "gy", None)
    field = P(None, "gx", "gy", None)
    return jax.shard_map(
        functools.partial(body, dims),
        mesh=mesh,
        in_specs=(field, cell, cell, cell, cell),
        out_specs=(field, P()),
        check_vma=False,
    )
```

time: 487 us -> 136 us (0.28); the launches traced: 478 us -> 134 us
  Pallas kernels: 0 us -> 128 us
  waiting for transfers between devices: 108 us -> 0 us
  starting transfers between devices: 88.9 us -> 0 us
  blocking collectives: 80.6 us -> 0 us
  other arithmetic: 77.1 us -> 0 us
  matrix products: 59.3 us -> 0 us
  local copies, waits for them, and re-layouts: 60.6 us -> 5.53 us
    pallas_call x0 -> x2, Pallas kernels: none -> 128 us  [the longest x1 118 us: body(): pl.pallas_call(functools.partial(respond_kernel, dims), out_shape=(jax.Sh...]
    ppermute x28 -> x0, waiting for transfers between devices: 108 us -> none  [the longest x14 57.8 us: padded_2(): after = lax.ppermute(first, axis, down)]
    ppermute x28 -> x0, starting transfers between devices: 88.9 us -> none  [the longest x14 65.8 us: padded_2(): before = lax.ppermute(last, axis, up)]
    psum x1 -> x0, blocking collectives: 80.6 us -> none  [body(): summed = lax.psum(gram, ('gx', 'gy'))]
    dot_general x66 -> x0, matrix products: 59.3 us -> none  [the longest x64 50 us: row_step(): jnp.dot(row, inverse, precision=lax.Precision.HIGHEST, preferred_element_...]
    add x5 -> x0, other arithmetic: 43.2 us -> none  [the longest x4 42 us: sweep(): return 0.2 * field + 0.8 * (rhs + total) / diag]
    dynamic_slice x64 -> x0, local copies, waits for them, and re-layouts: 37.6 us -> none  [row_step(): pivot = lax.dynamic_slice(lower, (index, index), (1, 1))]
    mul x1 -> x0, other arithmetic: 14.5 us -> none  [body(): responses = (sensitivity * adjoint).reshape(count, -1)]
  transfers between devices with their start and end apart: 28 -> 0, of which waited for: 26 -> 0; matrix products, arithmetic and copies ran while one was open for 0% -> 0% of each run, Pallas kernels for 0% -> 0%
where the time goes in v1:
time: 136 us; the launch traced here: 134 us
  Pallas kernels  128 us (94%)
  local copies, waits for them, and re-layouts  5.53 us (4%)
    pallas_call x1, Pallas kernels, body(): pl.pallas_call(functools.partial(respond_kernel, dims), out_shape=(jax.Sh...  118 us
    pallas_call x1, Pallas kernels, body(): pl.pallas_call(basis_kernel, grid=(wx,), out_shape=(jax.ShapeDtypeStruct(...  10.7 us
    unnamed x10, local copies, waits for them, and re-layouts  5.53 us

profile of v1, /device:TPU:1, one launch (start us, length us, event | category | flops | bytes accessed | tf_op | source)
XLA Modules:
  0.0 134.4 jit_solution(9139654417375480566)
XLA Ops:
  0.6 0.0 copy-start.1
  0.6 0.8 copy-done.1
  1.5 0.0 copy-start.2
  1.5 0.8 copy-done.2
  2.3 0.0 copy-start.3
  2.3 0.8 copy-done.3
  3.2 0.0 copy-start.4
  3.2 0.8 copy-done.4
  4.0 117.5 %shard_map.68 = (bf16[8,16,128,128]{3,2,1,0:T(8,128)(2,1)}, f32[32,128]{1,0:T(8,128)S(1)}) custom-call(bf16[64,8,16,128]{3,2,1,0:T(8,128)(2,1)} %probes.1, f32[8,16,128]{2,1,0:T(8,128)S(1)} %copy-done.1, f32[8,16,128]{2,1,0:T(8,128)S(1)} %copy-done.2, f32[8,16,128]{2,1,0:T(8,128)S(1)} %copy-done.3, f32[8,16,128]{2,1,0:T(8,128)S(1)} %copy-done.4), custom_call_target="tpu_custom_call" | custom-call | tf_op jit(solution)/shard_map/pallas_call | solution.py:297
  121.5 0.0 copy-start
  121.5 2.2 %copy-done = bf16[8,16,128,128]{3,2,1,0:T(8,128)(2,1)S(1)} copy-done((bf16[8,16,128,128]{3,2,1,0:T(8,128)(2,1)S(1)}, bf16[8,16,128,128]{3,2,1,0:T(8,128)(2,1)}, u32[]{:S(2)}) %copy-start) | copy-done | bytes 4194328
  123.7 10.7 %shard_map.69 = (f32[64,8,16,128]{3,2,1,0:T(8,128)}, f32[64,64]{1,0:T(8,128)}) custom-call(bf16[8,16,128,128]{3,2,1,0:T(8,128)(2,1)S(1)} %copy-done, f32[32,128]{1,0:T(8,128)S(1)} %get-tuple-element.5.gram_ref), custom_call_target="tpu_custom_call" | custom-call | tf_op jit(solution)/shard_map/pallas_call | solution.py:331
Async XLA Ops:
  0.6 0.8 copy-start.1
  1.5 0.8 copy-start.2
  2.3 0.8 copy-start.3
  3.2 0.8 copy-start.4
  121.5 2.2 %copy-start = (bf16[8,16,128,128]{3,2,1,0:T(8,128)(2,1)S(1)}, bf16[8,16,128,128]{3,2,1,0:T(8,128)(2,1)}, u32[]{:S(2)}) copy-start(bf16[8,16,128,128]{3,2,1,0:T(8,128)(2,1)} %get-tuple-element.4.y_ref) | copy-start | bytes 12582916

commit v2 on v1

v2 whole, which is shorter than its diff:
```python
import functools

import jax
import jax.numpy as jnp
from jax import lax
from jax.experimental import pallas as pl
from jax.experimental.pallas import tpu as pltpu
from jax.sharding import PartitionSpec as P

MESH = pl.DeviceIdType.MESH
GROUPS = 4
PANEL = 8


def remote(src, dst, send, recv, where):
    return pltpu.make_async_remote_copy(
        src_ref=src, dst_ref=dst, send_sem=send, recv_sem=recv, device_id=where, device_id_type=MESH
    )


def respond_kernel(
    dims,
    probes_hbm, perm_hbm, absorption_hbm, sensitivity_hbm, weight_hbm,
    y_hbm, gram_out,
    probes, perm, absorption, sensitivity, weight,
    raw, even, odd, rhs, y_out, stage, kpad, kface, khalo_x, khalo_y, sface, shalo_x, shalo_y,
    natural, spread, seed_row, product,
    slot_y, slot_x, slot_z,
    in_sem, out_sem, k_send, k_recv, s_send, s_recv, f_send, f_recv, r_send, r_recv,
):
    peers_x, peers_y, chips_x, chips_z = dims
    count, wx, wy, wz = probes.shape
    size = count // GROUPS
    tiles = size // 8
    gx, gy = lax.axis_index("gx"), lax.axis_index("gy")
    cx, cz = gx // chips_z, gx % chips_z

    x_before = ((gx + peers_x - 1) % peers_x, gy)
    x_after = ((gx + 1) % peers_x, gy)
    y_before = (gx, (gy + peers_y - 1) % peers_y)
    y_after = (gx, (gy + 1) % peers_y)
    other_y = [(gx, (gy + j) % peers_y) for j in range(1, peers_y)]
    other_x = [((cx + j) % chips_x * chips_z + cz, gy) for j in range(1, chips_x)]
    other_z = [(cx * chips_z + (cz + j) % chips_z, gy) for j in range(1, chips_z)]

    barrier = pltpu.get_barrier_semaphore()
    everyone = [x_before, x_after, y_before, y_after] + other_y + other_x + other_z
    for where in everyone:
        pl.semaphore_signal(barrier, inc=1, device_id=where, device_id_type=MESH)

    loads = [
        pltpu.make_async_copy(src, dst, in_sem.at[i])
        for i, (src, dst) in enumerate((
            (perm_hbm, perm), (absorption_hbm, absorption), (sensitivity_hbm, sensitivity), (weight_hbm, weight)
        ))
    ]

    def probe_load(g):
        at = pl.ds(g * size, size)
        return pltpu.make_async_copy(probes_hbm.at[at], probes.at[at], in_sem.at[4 + g])

    probe_load(0).start()
    loads[0].start()
    for g in range(1, GROUPS):
        probe_load(g).start()
    for load in loads[1:]:
        load.start()

    fields = (even, odd)

    def faces(e, g):
        mine = (fields[e % 2] if e else raw).at[g]
        sides = (
            (mine.at[wx, pl.ds(1, wy)], mine.at[0, pl.ds(1, wy)], x_after),
            (mine.at[1, pl.ds(1, wy)], mine.at[wx + 1, pl.ds(1, wy)], x_before),
            (mine.at[pl.ds(1, wx), wy], mine.at[pl.ds(1, wx), 0], y_after),
            (mine.at[pl.ds(1, wx), 1], mine.at[pl.ds(1, wx), wy + 1], y_before),
        )
        return [
            remote(src, dst, f_send.at[e % 2, g, i], f_recv.at[e % 2, g, i], where)
            for i, (src, dst, where) in enumerate(sides)
        ]

    def side_rows(pair, halo_x, halo_y, array, send, recv):
        return [
            remote(array.at[wx - 1], halo_x.at[0], send.at[0], recv.at[0], x_after),
            remote(array.at[0], halo_x.at[1], send.at[1], recv.at[1], x_before),
            remote(pair.at[1], halo_y.at[0], send.at[2], recv.at[2], y_after),
            remote(pair.at[0], halo_y.at[1], send.at[3], recv.at[3], y_before),
        ]

    def plane_of(g):
        def plane(x):
            def one(p, carry):
                stage[pl.ds(p, wy, stride=size), :] = probes[g * size + p, x].astype(jnp.float32)
                return carry

            lax.fori_loop(0, size, one, 0, unroll=True)
            raw[g, x + 1, pl.ds(1, wy)] = stage[...].reshape(wy, size, wz)

        return plane

    def outer_planes(g):
        plane = plane_of(g)

        def body(i, carry):
            plane(i * (wx - 1))
            return carry

        probe_load(g).wait()
        lax.fori_loop(0, 2, body, 0)

    def inner_planes(g):
        plane = plane_of(g)

        def body(x, carry):
            plane(x)
            return carry

        lax.fori_loop(1, wx - 1, body, 0)

    def send_x(g):
        for copy in faces(0, g)[:2]:
            copy.start()

    def send_y(g):
        for copy in faces(0, g)[2:]:
            copy.start()

    loads[0].wait()
    kface[0] = perm[:, 0, :]
    kface[1] = perm[:, wy - 1, :]
    k_copies = side_rows(kface, khalo_x, khalo_y, perm, k_send, k_recv)

    outer_planes(0)
    pl.semaphore_wait(barrier, len(everyone))
    for copy in k_copies:
        copy.start()
    send_x(0)
    outer_planes(1)
    send_x(1)
    inner_planes(0)
    send_y(0)
    inner_planes(1)
    send_y(1)

    for load in loads[1:]:
        load.wait()
    for copy in k_copies:
        copy.wait()

    has_x_low = jnp.where(gx > 0, 1.0, 0.0).astype(jnp.float32)
    has_x_high = jnp.where(gx < peers_x - 1, 1.0, 0.0).astype(jnp.float32)
    has_y_low = jnp.where(gy > 0, 1.0, 0.0).astype(jnp.float32)
    has_y_high = jnp.where(gy < peers_y - 1, 1.0, 0.0).astype(jnp.float32)

    center = perm[...]
    kpad[pl.ds(1, wx), pl.ds(8, wy), :] = center
    kpad[0, pl.ds(8, wy), :] = khalo_x[0] * has_x_low
    kpad[wx + 1, pl.ds(8, wy), :] = khalo_x[1] * has_x_high
    for x in range(wx):
        kpad[x + 1, 7:8, :] = khalo_y[0, x:x + 1, :] * has_y_low
        kpad[x + 1, wy + 8:wy + 9, :] = khalo_y[1, x:x + 1, :] * has_y_high
    lane = lax.broadcasted_iota(jnp.int32, (wx, wy, wz), 2)
    x_at = lax.broadcasted_iota(jnp.int32, (wx, wy, wz), 0)
    y_at = lax.broadcasted_iota(jnp.int32, (wx, wy, wz), 1)

    def turned(value, shift):
        flat = pltpu.roll(value.reshape(-1, wz), shift, 1)
        return flat.reshape(value.shape)

    x_low = 0.5 * (center + kpad[pl.ds(0, wx), pl.ds(8, wy), :])
    x_high = 0.5 * (center + kpad[pl.ds(2, wx), pl.ds(8, wy), :])
    y_low = 0.5 * (center + kpad[pl.ds(1, wx), pl.ds(7, wy), :])
    y_high = 0.5 * (center + kpad[pl.ds(1, wx), pl.ds(9, wy), :])
    z_low = 0.5 * (center + jnp.where(lane == 0, 0.0, turned(center, 1)))
    z_high = 0.5 * (center + jnp.where(lane == wz - 1, 0.0, turned(center, wz - 1)))
    diag = absorption[...] + x_low + x_high + y_low + y_high + z_low + z_high
    damp = 0.8 / diag
    seed = damp * sensitivity[...]
    natural[8] = seed
    sface[0] = seed[:, 0, :]
    sface[1] = seed[:, wy - 1, :]
    s_copies = side_rows(sface, shalo_x, shalo_y, natural.at[8], s_send, s_recv)
    for copy in s_copies:
        copy.start()
    for g in range(2, GROUPS):
        outer_planes(g)
        send_x(g)
    for g in range(2, GROUPS):
        inner_planes(g)
        send_y(g)
    natural[0] = damp * jnp.where(x_at == 0, x_low * has_x_low, x_low)
    natural[1] = damp * jnp.where(x_at == wx - 1, x_high * has_x_high, x_high)
    natural[2] = damp * jnp.where(y_at == 0, y_low * has_y_low, y_low)
    natural[3] = damp * jnp.where(y_at == wy - 1, y_high * has_y_high, y_high)
    natural[4] = damp * jnp.where(lane == 0, 0.0, z_low)
    natural[5] = damp * jnp.where(lane == wz - 1, 0.0, z_high)
    natural[6] = damp * weight[...]
    natural[7] = sensitivity[...]

    def widen(x, carry):
        for j in range(9):
            block = natural[j, x]
            for y in range(wy):
                row = jnp.broadcast_to(block[y:y + 1, :], (8, wz))
                if j < 8:
                    spread[j, x, y] = row
                else:
                    seed_row[x + 1, y + 1] = row
        return carry

    lax.fori_loop(0, wx, widen, 0)
    for copy in s_copies:
        copy.wait()
    for side in range(2):
        for y in range(wy):
            seed_row[side * (wx + 1), y + 1] = jnp.broadcast_to(shalo_x[side, y:y + 1, :], (8, wz))
        for x in range(wx):
            seed_row[x + 1, side * (wy + 1)] = jnp.broadcast_to(shalo_y[side, x:x + 1, :], (8, wz))

    def seeded(g, at_x, at_y, n):
        value = raw[g, at_x, at_y].reshape(n, tiles, 8, wz) * seed_row[at_x, at_y].reshape(n, 1, 8, wz)
        return value.reshape(n, size, wz)

    def inside(g, carry):
        def plane(x, carry):
            value = seeded(g, x + 1, pl.ds(1, wy), wy)
            even[g, x + 1, pl.ds(1, wy)] = value
            rhs[g, x] = value
            return carry

        lax.fori_loop(0, wx, plane, 0)
        return carry

    lax.fori_loop(0, GROUPS, inside, 0)

    def sweep(e, g, last):
        old, new = fields[e % 2], fields[(e + 1) % 2]
        shape = (wy, tiles, 8, wz)

        def plane(x, carry):
            def near(dx, dy):
                return old[g, x + 1 + dx, pl.ds(1 + dy, wy)].reshape(shape)

            def factor(j):
                return spread[j, x].reshape(wy, 1, 8, wz)

            here = near(0, 0)
            total = rhs[g, x].reshape(shape) + 0.2 * here
            total = total + factor(0) * near(-1, 0) + factor(1) * near(1, 0)
            total = total + factor(2) * near(0, -1) + factor(3) * near(0, 1)
            total = total + factor(4) * turned(here, 1) + factor(5) * turned(here, wz - 1)
            if last == 2:
                total = (total * factor(7)).reshape(wy, size, wz)
                high = total.astype(jnp.bfloat16)
                low = (total - high.astype(jnp.float32)).astype(jnp.bfloat16)
                y_out[x, :, pl.ds(2 * g * size, size), :] = high
                y_out[x, :, pl.ds((2 * g + 1) * size, size), :] = low
                return carry
            if last == 1:
                total = total * factor(6)
                rhs[g, x] = total.reshape(wy, size, wz)
            new[g, x + 1, pl.ds(1, wy)] = total.reshape(wy, size, wz)
            return carry

        lax.fori_loop(0, wx, plane, 0)

    def step(e, g):
        if e:
            for copy in faces(e - 1, g):
                copy.wait_send()
        for copy in faces(e, g):
            copy.wait_recv()
        if e == 0:
            for side in range(2):
                x, y = side * (wx + 1), side * (wy + 1)
                even[g, x, pl.ds(1, wy)] = seeded(g, x, pl.ds(1, wy), wy)
                even[g, pl.ds(1, wx), y] = seeded(g, pl.ds(1, wx), y, wx)
        sweep(e, g, 1 if e == 2 else 2 if e == 5 else 0)
        if e < 5:
            for copy in faces(e + 1, g):
                copy.start()

    def run(e):
        def body(g, carry):
            step(e, g)
            return carry
        lax.fori_loop(0, GROUPS, body, 0)

    for e in range(5):
        run(e)

    def y_write(g):
        at = pl.ds(2 * size * g, 2 * size)
        return pltpu.make_async_copy(y_out.at[:, :, at], y_hbm.at[:, :, at], out_sem.at[g])

    for g in range(GROUPS):
        step(5, g)
        for copy in faces(5, g):
            copy.wait_send()
        y_write(g).start()
        high_row = 2 * size * (g + 1)

        def add(x, acc):
            for y in range(0, wy, 2):
                both = jnp.concatenate([y_out[x, y, :high_row], y_out[x, y + 1, :high_row]], axis=1)
                acc = acc + lax.dot_general(
                    both, both[2 * size * g:], (((1,), (1,)), ((), ())), preferred_element_type=jnp.float32
                )
            return acc

        block = lax.fori_loop(0, wx, add, jnp.zeros((high_row, 2 * size), jnp.float32))
        product[:high_row, 2 * size * g:high_row] = block
        if g + 1 < GROUPS:
            product[high_row:, 2 * size * g:high_row] = jnp.zeros((2 * count - high_row, 2 * size), jnp.float32)

    folded = product[...].reshape(GROUPS, 2, size, 2 * count)
    folded = (folded[:, 0] + folded[:, 1]).reshape(count, 2 * count)
    twice = jnp.dot(
        folded, parts_of(2 * count, 2 * count, size, True),
        precision=lax.Precision.HIGHEST, preferred_element_type=jnp.float32,
    )
    half = count // 2
    first_half = lax.broadcasted_iota(jnp.int32, (half, 2 * count), 1) < count
    packed = jnp.where(first_half, twice[:half], twice[half:])
    base, sent = 0, []
    for slots, me, others in (
        (slot_y, gy, other_y), (slot_x, cx, other_x), (slot_z, cz, other_z)
    ):
        n = len(others) + 1
        slots[me] = packed
        copies = [
            remote(slots.at[me], slots.at[me], r_send.at[base + j], r_recv.at[base + j], where)
            for j, where in enumerate(others)
        ]
        for copy in copies:
            copy.start()
        sent += copies
        for copy in copies:
            copy.wait_recv()
        packed = slots[0]
        for j in range(1, n):
            packed = packed + slots[j]
        base += n - 1
    cells = float(wx * peers_x * wy * peers_y * wz)
    gram_out[...] = packed / cells
    for copy in sent:
        copy.wait_send()
    for g in range(GROUPS):
        y_write(g).wait()


def parts_of(height, width, size, from_parts):
    row, lane = (lax.broadcasted_iota(jnp.int32, (height, width), d) for d in (0, 1))
    part, number = (row, lane) if from_parts else (lane, row)
    count = width // 2
    of_part = part // (2 * size) * size + part % size
    return jnp.where(of_part == number % count, 1.0, 0.0).astype(jnp.float32)


def basis_kernel(y_hbm, gram_ref, q_ref, r_ref, y_ref, mix, stage, y_sem):
    count = q_ref.shape[0]
    half = count // 2
    size = count // GROUPS
    wy, wz = q_ref.shape[2], q_ref.shape[3]
    x = pl.program_id(0)

    @pl.when(x == 0)
    def _():
        y_read = pltpu.make_async_copy(y_hbm, y_ref, y_sem)
        y_read.start()
        packed = gram_ref[...]
        wide = (count, 2 * count)
        rows, lanes = (lax.broadcasted_iota(jnp.int32, wide, d) for d in (0, 1))
        upper = jnp.concatenate([packed, pltpu.roll(packed, count, 1)], axis=0)
        turned = jnp.transpose(jnp.concatenate([upper, upper], axis=0))[:count]
        whole = jnp.where(lanes // size >= rows // size, upper, turned)
        work = jnp.where(lanes < count, whole, jnp.where(lanes - count == rows, 1.0, 0.0))
        pivots, done = [], []
        for base in range(0, count, PANEL):
            height = count - base
            below = lax.broadcasted_iota(jnp.int32, (height, 2 * count), 0)
            columns = [
                jnp.broadcast_to(work[:, base + k:base + k + 1], (height, 2 * count)) for k in range(PANEL)
            ]
            for k in range(PANEL):
                pivot = columns[k][k:k + 1]
                pivots.append(pivot)
                inverse = 1.0 / pivot
                column = jnp.where(below > k, columns[k], 0.0)
                for m in range(k + 1, PANEL):
                    columns[m] = columns[m] - column * (columns[m][k:k + 1] * inverse)
                work = work - column * (work[k:k + 1] * inverse)
            done.append(work[:PANEL])
            work = work[PANEL:]
        work = jnp.concatenate(done, axis=0) * lax.rsqrt(jnp.concatenate(pivots, axis=0))
        r_ref[...] = jnp.where(lanes >= rows, work, 0.0)[:, :count]
        inverse = pltpu.roll(work, count, 1)[:, :count]
        high = inverse.astype(jnp.bfloat16)
        low = (inverse - high.astype(jnp.float32)).astype(jnp.bfloat16)
        place = parts_of(count, 2 * count, size, False).astype(jnp.bfloat16)
        mix[:, :2 * count] = jnp.dot(high, place, preferred_element_type=jnp.float32).astype(jnp.bfloat16)
        mix[:, 2 * count:] = jnp.dot(low, place, preferred_element_type=jnp.float32).astype(jnp.bfloat16)
        y_read.wait()

    weights = mix[...]
    for y in range(0, wy, 2):
        both = jnp.concatenate([y_ref[x, y], y_ref[x, y + 1]], axis=1)
        both = jnp.concatenate([both, both], axis=0)
        out = jnp.dot(weights, both, preferred_element_type=jnp.float32)
        stage[pl.ds(y, count, stride=wy), :] = out[:, :wz]
        stage[pl.ds(y + 1, count, stride=wy), :] = out[:, wz:]
    q_ref[:, 0] = stage[...].reshape(count, wy, wz)


def body(dims, probes, permeability, absorption, sensitivity, observe_weight):
    count, wx, wy, wz = probes.shape
    size = count // GROUPS
    peers_x, peers_y, chips_x, chips_z = dims
    f32 = jnp.float32
    vmem = pl.BlockSpec(memory_space=pltpu.VMEM)
    hops = peers_y - 1 + chips_x - 1 + chips_z - 1
    half = count // 2
    padded = pltpu.VMEM((GROUPS, wx + 2, wy + 2, size, wz), f32)
    responses, gram = pl.pallas_call(
        functools.partial(respond_kernel, dims),
        out_shape=(
            jax.ShapeDtypeStruct((wx, wy, 2 * count, wz), jnp.bfloat16),
            jax.ShapeDtypeStruct((half, 2 * count), f32),
        ),
        in_specs=[pl.BlockSpec(memory_space=pl.ANY)] * 5,
        out_specs=(pl.BlockSpec(memory_space=pl.ANY), vmem),
        scratch_shapes=[
            pltpu.VMEM((count, wx, wy, wz), jnp.bfloat16),
            pltpu.VMEM((wx, wy, wz), f32),
            pltpu.VMEM((wx, wy, wz), f32),
            pltpu.VMEM((wx, wy, wz), f32),
            pltpu.VMEM((wx, wy, wz), f32),
            padded,
            padded,
            padded,
            pltpu.VMEM((GROUPS, wx, wy, size, wz), f32),
            pltpu.VMEM((wx, wy, 2 * count, wz), jnp.bfloat16),
            pltpu.VMEM((wy * size, wz), f32),
            pltpu.VMEM((wx + 2, wy + 16, wz), f32),
            pltpu.VMEM((2, wx, wz), f32),
            pltpu.VMEM((2, wy, wz), f32),
            pltpu.VMEM((2, wx, wz), f32),
            pltpu.VMEM((2, wx, wz), f32),
            pltpu.VMEM((2, wy, wz), f32),
            pltpu.VMEM((2, wx, wz), f32),
            pltpu.VMEM((9, wx, wy, wz), f32),
            pltpu.VMEM((8, wx, wy, 8, wz), f32),
            pltpu.VMEM((wx + 2, wy + 2, 8, wz), f32),
            pltpu.VMEM((2 * count, 2 * count), f32),
            pltpu.VMEM((peers_y, half, 2 * count), f32),
            pltpu.VMEM((chips_x, half, 2 * count), f32),
            pltpu.VMEM((chips_z, half, 2 * count), f32),
            pltpu.SemaphoreType.DMA((4 + GROUPS,)),
            pltpu.SemaphoreType.DMA((GROUPS,)),
            pltpu.SemaphoreType.DMA((4,)),
            pltpu.SemaphoreType.DMA((4,)),
            pltpu.SemaphoreType.DMA((4,)),
            pltpu.SemaphoreType.DMA((4,)),
            pltpu.SemaphoreType.DMA((2, GROUPS, 4)),
            pltpu.SemaphoreType.DMA((2, GROUPS, 4)),
            pltpu.SemaphoreType.DMA((hops,)),
            pltpu.SemaphoreType.DMA((hops,)),
        ],
        compiler_params=pltpu.CompilerParams(
            collective_id=0, has_side_effects=True, vmem_limit_bytes=60 * 2**20
        ),
    )(probes, permeability, absorption, sensitivity, observe_weight)

    q_basis, r_factor = pl.pallas_call(
        basis_kernel,
        grid=(wx,),
        out_shape=(
            jax.ShapeDtypeStruct((count, wx, wy, wz), f32),
            jax.ShapeDtypeStruct((count, count), f32),
        ),
        in_specs=[
            pl.BlockSpec(memory_space=pl.ANY),
            pl.BlockSpec((half, 2 * count), lambda i: (0, 0)),
        ],
        out_specs=(
            pl.BlockSpec((count, 1, wy, wz), lambda i: (0, i, 0, 0)),
            pl.BlockSpec((count, count), lambda i: (0, 0)),
        ),
        scratch_shapes=[
            pltpu.VMEM((wx, wy, 2 * count, wz), jnp.bfloat16),
            pltpu.VMEM((count, 4 * count), jnp.bfloat16),
            pltpu.VMEM((count * wy, wz), f32),
            pltpu.SemaphoreType.DMA,
        ],
        compiler_params=pltpu.CompilerParams(vmem_limit_bytes=60 * 2**20),
    )(responses, gram)
    return q_basis, r_factor


def solution(mesh):
    peers_x, peers_y = mesh.shape["gx"], mesh.shape["gy"]
    chips_x = 4
    dims = (peers_x, peers_y, chips_x, peers_x // chips_x)
    cell = P("gx", "gy", None)
    field = P(None, "gx", "gy", None)
    return jax.shard_map(
        functools.partial(body, dims),
        mesh=mesh,
        in_specs=(field, cell, cell, cell, cell),
        out_specs=(field, P()),
        check_vma=False,
    )
```

time: 136 us -> 108 us (0.79)
  Pallas kernels: 128 us -> 107 us
  local copies, waits for them, and re-layouts: 5.53 us -> 0 us
    pallas_call x1, Pallas kernels: 118 us -> 99.1 us  [body(): pl.pallas_call(functools.partial(respond_kernel, dims), out_shape=(jax.Sh...]
    unnamed x10 -> x0, local copies, waits for them, and re-layouts: 5.53 us -> none
    pallas_call x1, Pallas kernels: 10.7 us -> 8.04 us  [body(): pl.pallas_call(basis_kernel, grid=(wx,), out_shape=(jax.ShapeDtypeStruct(...]
where the time goes in v2:
time: 108 us
  Pallas kernels  107 us (99%)
    pallas_call x1, Pallas kernels, body(): pl.pallas_call(functools.partial(respond_kernel, dims), out_shape=(jax.Sh...  99.1 us
    pallas_call x1, Pallas kernels, body(): pl.pallas_call(basis_kernel, grid=(wx,), out_shape=(jax.ShapeDtypeStruct(...  8.04 us

profile of v2, /device:TPU:1, one launch (start us, length us, event | category | flops | bytes accessed | tf_op | source)
XLA Modules:
  0.0 107.7 jit_solution(7363708979575906543)
XLA Ops:
  0.6 99.1 %shard_map.68 = (bf16[8,16,128,128]{3,2,1,0:T(8,128)(2,1)}, f32[32,128]{1,0:T(8,128)}) custom-call(bf16[64,8,16,128]{3,2,1,0:T(8,128)(2,1)} %probes_hbm.1, f32[8,16,128]{2,1,0:T(8,128)} %perm_hbm.1, f32[8,16,128]{2,1,0:T(8,128)} %absorption_hbm.1, f32[8,16,128]{2,1,0:T(8,128)} %sensitivity_hbm.1, f32[8,16,128]{2,1,0:T(8,128)} %weight_hbm.1), custom_call_target="tpu_custom_call" | custom-call | tf_op jit(solution)/shard_map/pallas_call | solution.py:426
  99.7 8.0 %shard_map.69 = (f32[64,8,16,128]{3,2,1,0:T(8,128)}, f32[64,64]{1,0:T(8,128)}) custom-call(bf16[8,16,128,128]{3,2,1,0:T(8,128)(2,1)} %get-tuple-element.4.y_hbm, f32[32,128]{1,0:T(8,128)} %get-tuple-element.5.gram_ref), custom_call_target="tpu_custom_call" | custom-call | tf_op jit(solution)/shard_map/pallas_call | solution.py:476

commit v3 on v2

--- a/solution.py
+++ b/solution.py
@@ -39,9 +39,12 @@
     x_after = ((gx + 1) % peers_x, gy)
     y_before = (gx, (gy + peers_y - 1) % peers_y)
     y_after = (gx, (gy + 1) % peers_y)
-    other_y = [(gx, (gy + j) % peers_y) for j in range(1, peers_y)]
-    other_x = [((cx + j) % chips_x * chips_z + cz, gy) for j in range(1, chips_x)]
-    other_z = [(cx * chips_z + (cz + j) % chips_z, gy) for j in range(1, chips_z)]
+    def far_first(n):
+        return sorted(range(1, n), key=lambda j: -min(j, n - j))
+
+    other_y = [(gx, (gy + j) % peers_y) for j in far_first(peers_y)]
+    other_x = [((cx + j) % chips_x * chips_z + cz, gy) for j in far_first(chips_x)]
+    other_z = [(cx * chips_z + (cz + j) % chips_z, gy) for j in far_first(chips_z)]
 
     barrier = pltpu.get_barrier_semaphore()
     everyone = [x_before, x_after, y_before, y_after] + other_y + other_x + other_z
@@ -239,7 +242,7 @@
         old, new = fields[e % 2], fields[(e + 1) % 2]
         shape = (wy, tiles, 8, wz)
 
-        def plane(x, carry):
+        def plane(x):
             def near(dx, dy):
                 return old[g, x + 1 + dx, pl.ds(1 + dy, wy)].reshape(shape)
 
@@ -253,18 +256,20 @@
             total = total + factor(4) * turned(here, 1) + factor(5) * turned(here, wz - 1)
             if last == 2:
                 total = (total * factor(7)).reshape(wy, size, wz)
-                high = total.astype(jnp.bfloat16)
-                low = (total - high.astype(jnp.float32)).astype(jnp.bfloat16)
-                y_out[x, :, pl.ds(2 * g * size, size), :] = high
-                y_out[x, :, pl.ds((2 * g + 1) * size, size), :] = low
-                return carry
+                high = total.astype(jnp.bfloat16).astype(jnp.float32)
+                parts = jnp.concatenate([high, total - high], axis=1).astype(jnp.bfloat16)
+                y_out[x, :, pl.ds(2 * g * size, 2 * size), :] = parts
+                return
             if last == 1:
                 total = total * factor(6)
                 rhs[g, x] = total.reshape(wy, size, wz)
             new[g, x + 1, pl.ds(1, wy)] = total.reshape(wy, size, wz)
+
+        def planes(x, carry):
+            plane(x)
             return carry
 
-        lax.fori_loop(0, wx, plane, 0)
+        lax.fori_loop(0, wx, planes, 0)
 
     def step(e, g):
         if e:
@@ -306,24 +311,21 @@
             for y in range(0, wy, 2):
                 both = jnp.concatenate([y_out[x, y, :high_row], y_out[x, y + 1, :high_row]], axis=1)
                 acc = acc + lax.dot_general(
-                    both, both[2 * size * g:], (((1,), (1,)), ((), ())), preferred_element_type=jnp.float32
+                    both[2 * size * g:], both, (((1,), (1,)), ((), ())), preferred_element_type=jnp.float32
                 )
             return acc
 
-        block = lax.fori_loop(0, wx, add, jnp.zeros((high_row, 2 * size), jnp.float32))
-        product[:high_row, 2 * size * g:high_row] = block
+        block = lax.fori_loop(0, wx, add, jnp.zeros((2 * size, high_row), jnp.float32))
+        product[2 * size * g:high_row, :high_row] = block
         if g + 1 < GROUPS:
-            product[high_row:, 2 * size * g:high_row] = jnp.zeros((2 * count - high_row, 2 * size), jnp.float32)
+            product[2 * size * g:high_row, high_row:] = jnp.zeros((2 * size, 2 * count - high_row), jnp.float32)
 
     folded = product[...].reshape(GROUPS, 2, size, 2 * count)
     folded = (folded[:, 0] + folded[:, 1]).reshape(count, 2 * count)
-    twice = jnp.dot(
-        folded, parts_of(2 * count, 2 * count, size, True),
-        precision=lax.Precision.HIGHEST, preferred_element_type=jnp.float32,
-    )
+    folded = folded + pltpu.roll(folded, 2 * count - size, 1)
     half = count // 2
-    first_half = lax.broadcasted_iota(jnp.int32, (half, 2 * count), 1) < count
-    packed = jnp.where(first_half, twice[:half], twice[half:])
+    first_half = lax.broadcasted_iota(jnp.int32, (half, 2 * count), 1) % (2 * size) < size
+    packed = jnp.where(first_half, folded[:half], pltpu.roll(folded[half:], size, 1))
     base, sent = 0, []
     for slots, me, others in (
         (slot_y, gy, other_y), (slot_x, cx, other_x), (slot_z, cz, other_z)
@@ -351,67 +353,77 @@
         y_write(g).wait()
 
 
-def parts_of(height, width, size, from_parts):
-    row, lane = (lax.broadcasted_iota(jnp.int32, (height, width), d) for d in (0, 1))
-    part, number = (row, lane) if from_parts else (lane, row)
-    count = width // 2
-    of_part = part // (2 * size) * size + part % size
-    return jnp.where(of_part == number % count, 1.0, 0.0).astype(jnp.float32)
-
-
-def basis_kernel(y_hbm, gram_ref, q_ref, r_ref, y_ref, mix, stage, y_sem):
+def basis_kernel(y_hbm, gram_ref, q_ref, r_ref, y_ref, mix, stage, y_sem, q_sem):
     count = q_ref.shape[0]
+    wx = q_ref.shape[1]
     half = count // 2
     size = count // GROUPS
     wy, wz = q_ref.shape[2], q_ref.shape[3]
-    x = pl.program_id(0)
-
-    @pl.when(x == 0)
-    def _():
-        y_read = pltpu.make_async_copy(y_hbm, y_ref, y_sem)
-        y_read.start()
-        packed = gram_ref[...]
-        wide = (count, 2 * count)
-        rows, lanes = (lax.broadcasted_iota(jnp.int32, wide, d) for d in (0, 1))
-        upper = jnp.concatenate([packed, pltpu.roll(packed, count, 1)], axis=0)
-        turned = jnp.transpose(jnp.concatenate([upper, upper], axis=0))[:count]
-        whole = jnp.where(lanes // size >= rows // size, upper, turned)
-        work = jnp.where(lanes < count, whole, jnp.where(lanes - count == rows, 1.0, 0.0))
-        pivots, done = [], []
-        for base in range(0, count, PANEL):
-            height = count - base
-            below = lax.broadcasted_iota(jnp.int32, (height, 2 * count), 0)
-            columns = [
-                jnp.broadcast_to(work[:, base + k:base + k + 1], (height, 2 * count)) for k in range(PANEL)
-            ]
-            for k in range(PANEL):
-                pivot = columns[k][k:k + 1]
-                pivots.append(pivot)
-                inverse = 1.0 / pivot
-                column = jnp.where(below > k, columns[k], 0.0)
-                for m in range(k + 1, PANEL):
-                    columns[m] = columns[m] - column * (columns[m][k:k + 1] * inverse)
-                work = work - column * (work[k:k + 1] * inverse)
-            done.append(work[:PANEL])
-            work = work[PANEL:]
-        work = jnp.concatenate(done, axis=0) * lax.rsqrt(jnp.concatenate(pivots, axis=0))
-        r_ref[...] = jnp.where(lanes >= rows, work, 0.0)[:, :count]
-        inverse = pltpu.roll(work, count, 1)[:, :count]
-        high = inverse.astype(jnp.bfloat16)
-        low = (inverse - high.astype(jnp.float32)).astype(jnp.bfloat16)
-        place = parts_of(count, 2 * count, size, False).astype(jnp.bfloat16)
-        mix[:, :2 * count] = jnp.dot(high, place, preferred_element_type=jnp.float32).astype(jnp.bfloat16)
-        mix[:, 2 * count:] = jnp.dot(low, place, preferred_element_type=jnp.float32).astype(jnp.bfloat16)
-        y_read.wait()
-
+
+    def y_read(n):
+        return pltpu.make_async_copy(y_hbm.at[n], y_ref.at[n], y_sem.at[n])
+
+    for n in range(wx):
+        y_read(n).start()
+    packed = gram_ref[...]
+    wide = (count, 2 * count)
+    rows, lanes = (lax.broadcasted_iota(jnp.int32, wide, d) for d in (0, 1))
+    lower = jnp.concatenate([packed, pltpu.roll(packed, 2 * count - size, 1)], axis=0)
+    pairs = lower.reshape(GROUPS, 1, size, 2 * count)
+    turned = jnp.transpose(jnp.concatenate([pairs, pairs], axis=1).reshape(2 * count, 2 * count))
+    turned = turned.reshape(GROUPS, 2, size, 2 * count)[:, 0].reshape(count, 2 * count)
+    in_gram = lanes % (2 * size) < size
+    number = lanes // (2 * size) * size + lanes % size
+    whole = jnp.where(lanes // (2 * size) <= rows // size, lower, turned)
+    work = jnp.where(in_gram, whole, jnp.where(number == rows, 1.0, 0.0))
+    pivots, done = [], []
+    for base in range(0, count, PANEL):
+        height = count - base
+        below = lax.broadcasted_iota(jnp.int32, (height, 2 * count), 0)
+        columns = [
+            jnp.broadcast_to(work[:, at:at + 1], (height, 2 * count))
+            for at in ((base + k) // size * 2 * size + (base + k) % size for k in range(PANEL))
+        ]
+        for k in range(PANEL):
+            pivot = columns[k][k:k + 1]
+            pivots.append(pivot)
+            inverse = 1.0 / pivot
+            column = jnp.where(below > k, columns[k], 0.0)
+            for m in range(k + 1, PANEL):
+                columns[m] = columns[m] - column * (columns[m][k:k + 1] * inverse)
+            work = work - column * (work[k:k + 1] * inverse)
+        done.append(work[:PANEL])
+        work = work[PANEL:]
+    work = jnp.concatenate(done, axis=0) * lax.rsqrt(jnp.concatenate(pivots, axis=0))
+    inverse = jnp.where(in_gram, pltpu.roll(work, 2 * count - size, 1), work)
+    high = inverse.astype(jnp.bfloat16)
+    mix[:, :2 * count] = high
+    mix[:, 2 * count:] = (inverse - high.astype(jnp.float32)).astype(jnp.bfloat16)
     weights = mix[...]
-    for y in range(0, wy, 2):
-        both = jnp.concatenate([y_ref[x, y], y_ref[x, y + 1]], axis=1)
-        both = jnp.concatenate([both, both], axis=0)
-        out = jnp.dot(weights, both, preferred_element_type=jnp.float32)
-        stage[pl.ds(y, count, stride=wy), :] = out[:, :wz]
-        stage[pl.ds(y + 1, count, stride=wy), :] = out[:, wz:]
-    q_ref[:, 0] = stage[...].reshape(count, wy, wz)
+
+    def q_write(x):
+        return pltpu.make_async_copy(stage.at[x].reshape(count, wy, wz), q_ref.at[:, x], q_sem.at[x])
+
+    def plane(x, carry):
+        y_read(x).wait()
+        for y in range(0, wy, 2):
+            both = jnp.concatenate([y_ref[x, y], y_ref[x, y + 1]], axis=1)
+            both = jnp.concatenate([both, both], axis=0)
+            out = jnp.dot(weights, both, preferred_element_type=jnp.float32)
+            stage[x, pl.ds(y, count, stride=wy), :] = out[:, :wz]
+            stage[x, pl.ds(y + 1, count, stride=wy), :] = out[:, wz:]
+        q_write(x).start()
+        return carry
+
+    lax.fori_loop(0, wx, plane, 0)
+    at, to = (lax.broadcasted_iota(jnp.int32, (2 * count, count), d) for d in (0, 1))
+    place = (at % (2 * size) < size) & (at // (2 * size) * size + at % size == to)
+    r_ref[...] = jnp.dot(
+        jnp.where(in_gram & (number >= rows), work, 0.0), jnp.where(place, 1.0, 0.0),
+        precision=lax.Precision.HIGHEST, preferred_element_type=jnp.float32,
+    )
+    for x in range(wx):
+        q_write(x).wait()
 
 
 def body(dims, probes, permeability, absorption, sensitivity, observe_weight):
@@ -475,24 +487,24 @@
 
     q_basis, r_factor = pl.pallas_call(
         basis_kernel,
-        grid=(wx,),
         out_shape=(
             jax.ShapeDtypeStruct((count, wx, wy, wz), f32),
             jax.ShapeDtypeStruct((count, count), f32),
         ),
         in_specs=[
             pl.BlockSpec(memory_space=pl.ANY),
-            pl.BlockSpec((half, 2 * count), lambda i: (0, 0)),
+            vmem,
         ],
         out_specs=(
-            pl.BlockSpec((count, 1, wy, wz), lambda i: (0, i, 0, 0)),
-            pl.BlockSpec((count, count), lambda i: (0, 0)),
+            pl.BlockSpec(memory_space=pl.ANY),
+            vmem,
         ),
         scratch_shapes=[
             pltpu.VMEM((wx, wy, 2 * count, wz), jnp.bfloat16),
             pltpu.VMEM((count, 4 * count), jnp.bfloat16),
-            pltpu.VMEM((count * wy, wz), f32),
-            pltpu.SemaphoreType.DMA,
+            pltpu.VMEM((wx, count * wy, wz), f32),
+            pltpu.SemaphoreType.DMA((wx,)),
+            pltpu.SemaphoreType.DMA((wx,)),
         ],
         compiler_params=pltpu.CompilerParams(vmem_limit_bytes=60 * 2**20),
     )(responses, gram)

time: 108 us -> 106 us (0.981)
  Pallas kernels: 107 us -> 105 us
    pallas_call x1, Pallas kernels: 8.04 us -> 6.86 us  [body(): pl.pallas_call(basis_kernel, out_shape=(jax.ShapeDtypeStruct((count, wx,...]
where the time goes in v3:
time: 106 us; the launch traced here: 105 us
  Pallas kernels  105 us (99%)
    pallas_call x1, Pallas kernels, body(): pl.pallas_call(functools.partial(respond_kernel, dims), out_shape=(jax.Sh...  98 us
    pallas_call x1, Pallas kernels, body(): pl.pallas_call(basis_kernel, out_shape=(jax.ShapeDtypeStruct((count, wx,...  6.86 us

profile of v3, /device:TPU:1, one launch (start us, length us, event | category | flops | bytes accessed | tf_op | source)
XLA Modules:
  0.0 105.5 jit_solution(12058924470391253810)
XLA Ops:
  0.6 98.0 %shard_map.68 = (bf16[8,16,128,128]{3,2,1,0:T(8,128)(2,1)}, f32[32,128]{1,0:T(8,128)}) custom-call(bf16[64,8,16,128]{3,2,1,0:T(8,128)(2,1)} %probes_hbm.1, f32[8,16,128]{2,1,0:T(8,128)} %perm_hbm.1, f32[8,16,128]{2,1,0:T(8,128)} %absorption_hbm.1, f32[8,16,128]{2,1,0:T(8,128)} %sensitivity_hbm.1, f32[8,16,128]{2,1,0:T(8,128)} %weight_hbm.1), custom_call_target="tpu_custom_call" | custom-call | tf_op jit(solution)/shard_map/pallas_call | solution.py:438
  98.6 6.9 %shard_map.69 = (f32[64,8,16,128]{3,2,1,0:T(8,128)}, f32[64,64]{1,0:T(8,128)}) custom-call(bf16[8,16,128,128]{3,2,1,0:T(8,128)(2,1)} %get-tuple-element.4.y_hbm, f32[32,128]{1,0:T(8,128)} %get-tuple-element.5.gram_ref), custom_call_target="tpu_custom_call" | custom-call | tf_op jit(solution)/shard_map/pallas_call | solution.py:488

commit v4 on v3

--- a/solution.py
+++ b/solution.py
@@ -238,7 +238,16 @@
 
     lax.fori_loop(0, GROUPS, inside, 0)
 
-    def sweep(e, g, last):
+    def inner(act, start):
+        return lax.fori_loop(1, wx - 1, act, start)
+
+    def outer(act, start):
+        return lax.fori_loop(0, 2, lambda i, carry: act(i * (wx - 1), carry), start)
+
+    def every(act, start):
+        return lax.fori_loop(0, wx, act, start)
+
+    def sweep(e, g, last, over):
         old, new = fields[e % 2], fields[(e + 1) % 2]
         shape = (wy, tiles, 8, wz)
 
@@ -269,7 +278,7 @@
             plane(x)
             return carry
 
-        lax.fori_loop(0, wx, planes, 0)
+        over(planes, 0)
 
     def step(e, g):
         if e:
@@ -282,10 +291,9 @@
                 x, y = side * (wx + 1), side * (wy + 1)
                 even[g, x, pl.ds(1, wy)] = seeded(g, x, pl.ds(1, wy), wy)
                 even[g, pl.ds(1, wx), y] = seeded(g, pl.ds(1, wx), y, wx)
-        sweep(e, g, 1 if e == 2 else 2 if e == 5 else 0)
-        if e < 5:
-            for copy in faces(e + 1, g):
-                copy.start()
+        sweep(e, g, 1 if e == 2 else 0, every)
+        for copy in faces(e + 1, g):
+            copy.start()
 
     def run(e):
         def body(g, carry):
@@ -300,11 +308,7 @@
         at = pl.ds(2 * size * g, 2 * size)
         return pltpu.make_async_copy(y_out.at[:, :, at], y_hbm.at[:, :, at], out_sem.at[g])
 
-    for g in range(GROUPS):
-        step(5, g)
-        for copy in faces(5, g):
-            copy.wait_send()
-        y_write(g).start()
+    def gram_rows(g, over):
         high_row = 2 * size * (g + 1)
 
         def add(x, acc):
@@ -315,10 +319,28 @@
                 )
             return acc
 
-        block = lax.fori_loop(0, wx, add, jnp.zeros((2 * size, high_row), jnp.float32))
-        product[2 * size * g:high_row, :high_row] = block
+        return over(add, jnp.zeros((2 * size, high_row), jnp.float32))
+
+    for g in range(GROUPS):
+        for copy in faces(4, g):
+            copy.wait_send()
+        for copy in faces(5, g)[2:]:
+            copy.wait_recv()
+        sweep(5, g, 2, inner)
+        high_row = 2 * size * (g + 1)
+        product[2 * size * g:high_row, :high_row] = gram_rows(g, inner)
         if g + 1 < GROUPS:
             product[2 * size * g:high_row, high_row:] = jnp.zeros((2 * size, 2 * count - high_row), jnp.float32)
+    for g in range(GROUPS):
+        for copy in faces(5, g)[:2]:
+            copy.wait_recv()
+        sweep(5, g, 2, outer)
+        y_write(g).start()
+        high_row = 2 * size * (g + 1)
+        product[2 * size * g:high_row, :high_row] += gram_rows(g, outer)
+    for g in range(GROUPS):
+        for copy in faces(5, g):
+            copy.wait_send()
 
     folded = product[...].reshape(GROUPS, 2, size, 2 * count)
     folded = (folded[:, 0] + folded[:, 1]).reshape(count, 2 * count)

time: 106 us -> 104 us (0.981)
  Pallas kernels: 105 us -> 103 us
    pallas_call x1, Pallas kernels: 98 us -> 95.9 us  [body(): pl.pallas_call(functools.partial(respond_kernel, dims), out_shape=(jax.Sh...]
where the time goes in v4:
time: 104 us; the launch traced here: 103 us
  Pallas kernels  103 us (99%)
    pallas_call x1, Pallas kernels, body(): pl.pallas_call(functools.partial(respond_kernel, dims), out_shape=(jax.Sh...  95.9 us
    pallas_call x1, Pallas kernels, body(): pl.pallas_call(basis_kernel, out_shape=(jax.ShapeDtypeStruct((count, wx,...  6.85 us

profile of v4, /device:TPU:1, one launch (start us, length us, event | category | flops | bytes accessed | tf_op | source)
XLA Modules:
  0.0 103.4 jit_solution(12795771410705809735)
XLA Ops:
  0.6 95.9 %shard_map.68 = (bf16[8,16,128,128]{3,2,1,0:T(8,128)(2,1)}, f32[32,128]{1,0:T(8,128)}) custom-call(bf16[64,8,16,128]{3,2,1,0:T(8,128)(2,1)} %probes_hbm.1, f32[8,16,128]{2,1,0:T(8,128)} %perm_hbm.1, f32[8,16,128]{2,1,0:T(8,128)} %absorption_hbm.1, f32[8,16,128]{2,1,0:T(8,128)} %sensitivity_hbm.1, f32[8,16,128]{2,1,0:T(8,128)} %weight_hbm.1), custom_call_target="tpu_custom_call" | custom-call | tf_op jit(solution)/shard_map/pallas_call | solution.py:460
  96.6 6.9 %shard_map.69 = (f32[64,8,16,128]{3,2,1,0:T(8,128)}, f32[64,64]{1,0:T(8,128)}) custom-call(bf16[8,16,128,128]{3,2,1,0:T(8,128)(2,1)} %get-tuple-element.4.y_hbm, f32[32,128]{1,0:T(8,128)} %get-tuple-element.5.gram_ref), custom_call_target="tpu_custom_call" | custom-call | tf_op jit(solution)/shard_map/pallas_call | solution.py:510

commit v5 on v4

--- a/solution.py
+++ b/solution.py
@@ -242,7 +242,7 @@
         return lax.fori_loop(1, wx - 1, act, start)
 
     def outer(act, start):
-        return lax.fori_loop(0, 2, lambda i, carry: act(i * (wx - 1), carry), start)
+        return lax.fori_loop(0, 2, lambda i, carry: act(i * (wx - 1), carry), start, unroll=True)
 
     def every(act, start):
         return lax.fori_loop(0, wx, act, start)

time: 104 us -> 102 us (0.981)
    pallas_call x1, Pallas kernels: 95.9 us -> 94.7 us  [body(): pl.pallas_call(functools.partial(respond_kernel, dims), out_shape=(jax.Sh...]
where the time goes in v5:
time: 102 us
  Pallas kernels  102 us (100%)
    pallas_call x1, Pallas kernels, body(): pl.pallas_call(functools.partial(respond_kernel, dims), out_shape=(jax.Sh...  94.7 us
    pallas_call x1, Pallas kernels, body(): pl.pallas_call(basis_kernel, out_shape=(jax.ShapeDtypeStruct((count, wx,...  6.85 us

profile of v5, /device:TPU:1, one launch (start us, length us, event | category | flops | bytes accessed | tf_op | source)
XLA Modules:
  0.0 102.2 jit_solution(12939058896807445318)
XLA Ops:
  0.6 94.7 %shard_map.68 = (bf16[8,16,128,128]{3,2,1,0:T(8,128)(2,1)}, f32[32,128]{1,0:T(8,128)}) custom-call(bf16[64,8,16,128]{3,2,1,0:T(8,128)(2,1)} %probes_hbm.1, f32[8,16,128]{2,1,0:T(8,128)} %perm_hbm.1, f32[8,16,128]{2,1,0:T(8,128)} %absorption_hbm.1, f32[8,16,128]{2,1,0:T(8,128)} %sensitivity_hbm.1, f32[8,16,128]{2,1,0:T(8,128)} %weight_hbm.1), custom_call_target="tpu_custom_call" | custom-call | tf_op jit(solution)/shard_map/pallas_call | solution.py:460
  95.4 6.9 %shard_map.69 = (f32[64,8,16,128]{3,2,1,0:T(8,128)}, f32[64,64]{1,0:T(8,128)}) custom-call(bf16[8,16,128,128]{3,2,1,0:T(8,128)(2,1)} %get-tuple-element.4.y_hbm, f32[32,128]{1,0:T(8,128)} %get-tuple-element.5.gram_ref), custom_call_target="tpu_custom_call" | custom-call | tf_op jit(solution)/shard_map/pallas_call | solution.py:510
